TPU v7x, 256 devices: a whole 4x4x8 slice. The times are simulated.
256 devices in a mesh: pairs: 64 (over z, x, core), mp: 4 (over y).
Axes of the slice: x: 4, y: 4, z: 8, core: 2. Of those that a mesh axis runs over, the one named last changes fastest.
Arguments:
- embeddings: bfloat16 [128, 128, 5120], P('pairs', None, 'mp'), may hold values from -12 to 12
- cotangent: bfloat16 [128, 128, 5120], P('pairs', None, 'mp'), may hold values from -6 to 6
- w_qk: bfloat16 [5120, 512], P('mp'), may hold values from -0.078125 to 0.078125
- w_value: bfloat16 [5120, 512], P('mp'), may hold values from -0.078125 to 0.078125
- w_out: bfloat16 [512, 5120], P(None, 'mp'), may hold values from -0.25 to 0.25
- lengths: int32 [128], replicated, may hold values from 16 to 128
- pair_list: int32 [1024, 2], replicated, may hold values from 0 to 127, as said below
Outputs:
- attended: bfloat16 [128, 128, 5120], P('pairs', None, 'mp')
- grad_qk: float32 [5120, 512], P('mp', 'pairs')
- grad_value: float32 [5120, 512], P('mp', 'pairs')
Inputs may be any that keep to these rules, and one draw needn't show every extreme that they name: `pair_list`: protein p belongs to owner p // 2. The pairs in rows w * 16 to (w + 1) * 16 - 1 go to worker w; the 32 proteins named in one worker's pairs belong to 32 different owners.
All inputs are finite; a program needn't handle non-finite values.
Results may differ from a plain program's by a relative error of at most 0.024.
The roundings to bfloat16 on the way count: a program that leaves them out, or rounds other values in their place, can miss the bound.
Values may be sent and summed in bfloat16 or wider, within the bound.
A program may use at most 128 MiB of HBM per device.

v0:
```python
import jax
import jax.numpy as jnp
from jax import lax
from jax.sharding import PartitionSpec as P

HDIM = 64


def pair_attend(key_a, key_b, value_a, value_b, length_a, length_b):
    crop = key_a.shape[0]
    width = key_a.shape[1]
    heads = width // HDIM
    qa = key_a.reshape(crop, heads, HDIM)
    qb = key_b.reshape(crop, heads, HDIM)
    va = value_a.reshape(crop, heads, HDIM)
    vb = value_b.reshape(crop, heads, HDIM)
    scores = jnp.einsum("rhd,chd->hrc", qa, qb, precision=lax.Precision.HIGHEST) * HDIM ** (-0.5)
    places = jnp.arange(crop, dtype=jnp.int32)
    column_ok = places[None, None, :] < length_b
    row_ok = places[None, :, None] < length_a
    by_rows = jax.nn.softmax(jnp.where(column_ok, scores, -1000000000.0), axis=2)
    by_columns = jax.nn.softmax(jnp.where(row_ok, scores, -1000000000.0), axis=1)
    out_a = jnp.einsum("hrc,chd->rhd", by_rows, vb, precision=lax.Precision.HIGHEST).reshape(
        crop, width
    )
    out_b = jnp.einsum("hrc,rhd->chd", by_columns, va, precision=lax.Precision.HIGHEST).reshape(
        crop, width
    )
    return (out_a, out_b)


def pair_grads(key_a, key_b, value_a, value_b, length_a, length_b, grad_a, grad_b):

    def local(ka, kb, va, vb):
        return pair_attend(ka, kb, va, vb, length_a, length_b)

    primal, pull = jax.vjp(local, key_a, key_b, value_a, value_b)
    return pull((grad_a, grad_b))


def on_device(embeddings, cotangent, w_qk, w_value, w_out, lengths, pair_list):
    owned, crop, width = embeddings.shape
    inner = w_qk.shape[1]
    groups = lax.axis_size("mp")
    group_cols = inner // groups
    rows = owned * crop
    flat = embeddings.reshape(rows, width)
    stacked = jnp.stack(
        (w_qk.reshape(width, groups, group_cols), w_value.reshape(width, groups, group_cols)),
        axis=2,
    )
    stacked = stacked.reshape(width, 2 * inner)
    partial_kv = jnp.dot(flat, stacked, preferred_element_type=jnp.float32)
    key_value = lax.psum_scatter(partial_kv, "mp", scatter_dimension=1, tiled=True).astype(
        jnp.bfloat16
    )
    key_value = key_value.reshape(owned, crop, 2 * group_cols)
    me = lax.axis_index("pairs")
    workers = lax.axis_size("pairs")
    per_worker = pair_list.shape[0] // workers
    my_lengths = lax.dynamic_slice_in_dim(lengths, me * owned, owned, 0)
    rows_ok = (jnp.arange(crop, dtype=jnp.int32)[None, :] < my_lengths[:, None]).astype(
        jnp.float32
    )[:, :, None]
    partial_back = lax.dot_general(
        cotangent.reshape(rows, width),
        w_out,
        (((1,), (1,)), ((), ())),
        preferred_element_type=jnp.float32,
    )
    head_back = (
        lax.psum_scatter(partial_back.astype(jnp.bfloat16), "mp", scatter_dimension=1, tiled=True)
        .astype(jnp.float32)
        .reshape(owned, crop, group_cols)
    )
    hidden_grad = (head_back * rows_ok).astype(jnp.bfloat16)
    owner_of = pair_list // owned
    local_of = pair_list % owned
    worker_of = jnp.broadcast_to(
        (jnp.arange(pair_list.shape[0], dtype=jnp.int32) // per_worker)[:, None], pair_list.shape
    )
    need = jnp.full((workers, workers), -1, jnp.int32).at[worker_of, owner_of].set(local_of)
    my_need = lax.dynamic_index_in_dim(need, me, 1, keepdims=False)
    used = (my_need >= 0)[:, None, None]
    safe_need = jnp.maximum(my_need, 0)
    outgoing_kv = jnp.where(
        used, jnp.take(key_value, safe_need, axis=0), jnp.zeros((), jnp.bfloat16)
    )
    outgoing_grad = jnp.where(
        used, jnp.take(hidden_grad, safe_need, axis=0), jnp.zeros((), jnp.bfloat16)
    )
    mine = lax.dynamic_slice_in_dim(pair_list, me * per_worker, per_worker, 0)
    slot_a = mine[:, 0] // owned
    slot_b = mine[:, 1] // owned
    length_a = lengths[mine[:, 0]]
    length_b = lengths[mine[:, 1]]
    arrived = lax.all_to_all(outgoing_kv, "pairs", split_axis=0, concat_axis=0, tiled=True)
    both_a = arrived[slot_a].astype(jnp.float32)
    both_b = arrived[slot_b].astype(jnp.float32)
    out_a, out_b = jax.vmap(pair_attend)(
        both_a[:, :, :group_cols],
        both_b[:, :, :group_cols],
        both_a[:, :, group_cols:],
        both_b[:, :, group_cols:],
        length_a,
        length_b,
    )
    slots = jnp.zeros((workers, crop, group_cols), jnp.float32)
    returned = lax.all_to_all(
        slots.at[slot_a].add(out_a).at[slot_b].add(out_b).astype(jnp.bfloat16),
        "pairs",
        split_axis=0,
        concat_axis=0,
        tiled=True,
    ).astype(jnp.float32)
    grads_in = lax.all_to_all(outgoing_grad, "pairs", split_axis=0, concat_axis=0, tiled=True)
    both_a = arrived[slot_a].astype(jnp.float32)
    both_b = arrived[slot_b].astype(jnp.float32)
    dka, dkb, dva, dvb = jax.vmap(pair_grads)(
        both_a[:, :, :group_cols],
        both_b[:, :, :group_cols],
        both_a[:, :, group_cols:],
        both_b[:, :, group_cols:],
        length_a,
        length_b,
        grads_in[slot_a].astype(jnp.float32),
        grads_in[slot_b].astype(jnp.float32),
    )
    slots = jnp.zeros((workers, crop, 2 * group_cols), jnp.float32)
    slots = slots.at[slot_a].add(jnp.concatenate((dka, dva), axis=2))
    grad_returned = lax.all_to_all(
        slots.at[slot_b].add(jnp.concatenate((dkb, dvb), axis=2)).astype(jnp.bfloat16),
        "pairs",
        split_axis=0,
        concat_axis=0,
        tiled=True,
    ).astype(jnp.float32)
    picker = (my_need[None, :] == jnp.arange(owned, dtype=jnp.int32)[:, None]).astype(jnp.float32)
    summed = jnp.einsum("pw,wlc->plc", picker, returned, precision=lax.Precision.HIGHEST)
    hidden = (summed * rows_ok).astype(jnp.bfloat16)
    all_heads = lax.all_gather(hidden, "mp", axis=2, tiled=True)
    attended = jnp.dot(all_heads.reshape(rows, inner), w_out, preferred_element_type=jnp.float32)
    attended = attended.astype(jnp.bfloat16).reshape(owned, crop, width)
    grad_sum = jnp.einsum(
        "pw,wlc->plc", picker, grad_returned, precision=lax.Precision.HIGHEST
    ).astype(jnp.bfloat16)
    all_grads = lax.all_gather(grad_sum, "mp", axis=2, tiled=True).reshape(rows, 2 * inner)
    weight_terms = lax.dot_general(
        flat, all_grads, (((0,), (0,)), ((), ())), preferred_element_type=jnp.float32
    )
    weight_terms = weight_terms.reshape(width, groups, 2, group_cols)
    term_qk = weight_terms[:, :, 0, :].reshape(width, inner)
    term_value = weight_terms[:, :, 1, :].reshape(width, inner)
    grad_qk, grad_value = (
        lax.psum_scatter(term_qk, "pairs", scatter_dimension=1, tiled=True),
        lax.psum_scatter(term_value, "pairs", scatter_dimension=1, tiled=True),
    )
    return (attended, grad_qk, grad_value)


def solution(mesh):
    in_specs = (
        P("pairs", None, "mp"),
        P("pairs", None, "mp"),
        P("mp", None),
        P("mp", None),
        P(None, "mp"),
        P(),
        P(),
    )
    out_specs = (P("pairs", None, "mp"), P("mp", "pairs"), P("mp", "pairs"))
    return jax.shard_map(
        on_device, mesh=mesh, in_specs=in_specs, out_specs=out_specs, check_vma=False
    )
```

profile of v0, /device:TPU:6, one launch (start us, length us, event | category | flops | bytes accessed | tf_op | source)
XLA Modules:
  0.0 699.9 jit_solution(7606829669265826412)
XLA Ops:
  8.9 2.4 copy.96
  13.0 1.9 convolution_bitcast_fusion
  16.2 8.1 %scatter_custom_fusion.4 = s32[4096]{0:T(1024)S(1)} fusion(s32[2048]{0:T(1024)S(1)} %reshape.376, s32[2048]{0:T(1024)S(1)} %reshape.378, s32[]{:T(128)} %constant.109.clone.1), kind=kCustom, calls=%fused_computation.62 | custom fusion | bytes 16388
  24.8 19.3 %reduce-scatter.5.cloned.1.call-done = f32[256,256]{0,1:T(8,128)} async-done(((f32[256,1024]{0,1:T(8,128)}), f32[256,256]{0,1:T(8,128)}) %reduce-scatter.5.cloned.1.call-update) | async-done | bytes 262160 | tf_op jit(solution)/shard_map/reduce_scatter | solution.py:54
  45.1 2.8 gather_fusion
  47.9 4.0 select_select_fusion
  51.9 11.5 %all-to-all-start = ((bf16[64,128,256]{2,1,0:T(8,128)(2,1)}), bf16[64,128,256]{2,1,0:T(8,128)(2,1)}, u32[]{:S(2)}, u32[]{:S(2)}) async-start(bf16[64,128,256]{2,1,0:T(8,128)(2,1)} %select_select_fusion), calls=%async_computation.1 | async-start | bytes 8388608 | tf_op jit(solution)/shard_map/all_to_all | solution.py:97
  65.0 94.3 %all-to-all-done = bf16[64,128,256]{2,1,0:T(8,128)(2,1)} async-done(((bf16[64,128,256]{2,1,0:T(8,128)(2,1)}), bf16[64,128,256]{2,1,0:T(8,128)(2,1)}, u32[]{:S(2)}, u32[]{:S(2)}) %all-to-all-start) | async-done | bytes 4194336 | tf_op jit(solution)/shard_map/all_to_all | solution.py:97
  159.3 2.8 gather_fusion.3
  163.5 2.8 gather_fusion.1
  169.4 2.6 select_reduce_fusion
  173.8 2.6 fusion.10
  176.4 2.5 copy.103
  179.0 2.1 copy.98
  181.1 4.7 fusion.8
  187.3 2.5 broadcast_in_dim.160
  189.8 3.4 scatter_fusion
  193.2 3.4 scatter_fusion.1
  196.7 3.9 convert_element_type.42
  200.6 5.4 all-to-all-start.1
  206.0 2.3 convolution_convert_fusion.1
  210.3 22.8 %reduce-scatter.7.cloned.1.call-done = bf16[128,256]{1,0:T(8,128)(2,1)} async-done(((bf16[512,256]{1,0:T(8,128)(2,1)}), bf16[128,256]{1,0:T(8,128)(2,1)}) %reduce-scatter.7.cloned.1.call-update) | async-done | bytes 65552
  234.7 22.6 %all-to-all-done.1 = bf16[64,128,128]{2,1,0:T(8,128)(2,1)S(1)} async-done(((bf16[64,128,128]{2,1,0:T(8,128)(2,1)}), bf16[64,128,128]{2,1,0:T(8,128)(2,1)S(1)}, u32[]{:S(2)}, u32[]{:S(2)}) %all-to-all-start.1) | async-done | bytes 2097184 | tf_op jit(solution)/shard_map/all_to_all | solution.py:109
  259.7 2.3 select_select_fusion.1
  262.0 5.5 all-to-all-start.2
  267.5 8.7 %all-reduce.5.cloned.1.call-start = ((), (), s32[]{:S(2)}) async-start(), calls=%async_computation.8 | async-start | bytes 10485760
  277.5 41.3 %all-to-all-done.2 = bf16[64,128,128]{2,1,0:T(8,128)(2,1)S(1)} async-done(((bf16[64,128,128]{2,1,0:T(8,128)(2,1)}), bf16[64,128,128]{2,1,0:T(8,128)(2,1)S(1)}, u32[]{:S(2)}, u32[]{:S(2)}) %all-to-all-start.2) | async-done | bytes 2097184 | tf_op jit(solution)/shard_map/all_to_all | solution.py:116
  321.7 2.2 copy.107
  323.9 3.1 fusion.42
  327.0 3.4 fusion.7
  330.3 3.1 gather_fusion.6
  333.5 2.1 copy.106
  335.5 4.2 multiply_reduce_fusion.1
  339.9 2.6 add_multiply_fusion
  342.5 2.1 fusion.44
  344.6 3.3 fusion.43
  347.8 3.5 fusion.9
  351.3 2.7 copy.112
  361.7 4.3 broadcast_in_dim.168
  366.0 5.4 scatter_fusion.2
  371.4 4.6 scatter_fusion.3
  376.0 4.0 convert_element_type.48
  380.0 101.6 %all_to_all.20 = bf16[64,128,256]{2,1,0:T(8,128)(2,1)S(1)} all-to-all(bf16[64,128,256]{2,1,0:T(8,128)(2,1)S(1)} %convert_element_type.48), channel_id=1, replica_groups=mesh['pairs'=64,'mp'=4] {'pairs'}, dimensions={0} | all-to-all | bytes 8388608 | tf_op jit(solution)/shard_map/all_to_all | solution.py:131
  481.6 2.4 fusion.4
  484.0 10.5 %all_gather.7 = bf16[2,128,1024]{2,0,1:T(2,128)(2,1)S(1)} all-gather(bf16[2,128,256]{2,0,1:T(2,128)(2,1)S(1)} %fusion.4), channel_id=1, replica_groups=mesh['pairs'=64,'mp'=4] {'mp'}, dimensions={2}, use_global_device_ids=true | all-gather | bytes 655360 | tf_op jit(solution)/shard_map/all_gather | solution.py:147
  495.4 2.7 fusion.39
  500.0 11.5 %all_gather.6 = bf16[2,128,512]{2,1,0:T(8,128)(2,1)S(1)} all-gather(bf16[2,128,128]{2,1,0:T(8,128)(2,1)S(1)} %get-tuple-element.22), channel_id=1, replica_groups=mesh['pairs'=64,'mp'=4] {'mp'}, dimensions={2}, use_global_device_ids=true | all-gather | bytes 327680 | tf_op jit(solution)/shard_map/all_gather | solution.py:141
  512.8 177.5 %all-reduce.5.cloned.1.call-done = (f32[1280,512]{0,1:T(8,128)}, f32[1280,512]{0,1:T(8,128)}) async-done(((f32[1280,512]{0,1:T(8,128)}, f32[1280,512]{0,1:T(8,128)}), (f32[1280,512]{0,1:T(8,128)}, f32[1280,512]{0,1:T(8,128)})) %all-reduce.5.cloned.1.call-update) | async-done | bytes 5242896
  (154 shorter events, 39.5 us)
Async XLA Ops:
  7.2 198.9 %copy-start = (bf16[512,1280]{1,0:T(8,128)(2,1)S(1)}, bf16[512,1280]{1,0:T(8,128)(2,1)}, u32[]{:S(2)}) copy-start(bf16[512,1280]{1,0:T(8,128)(2,1)} %param.11) | copy-start | bytes 3932164
  7.2 36.8 %reduce-scatter.5.cloned.1.call-start = ((), (), s32[]{:S(2)}) async-start(), calls=%async_computation.6 | async-start | bytes 1310720 | tf_op jit(solution)/shard_map/reduce_scatter | solution.py:54
  11.4 1.6 copy-start.15
  13.0 2.0 copy-start.32
  13.0 2.0 copy-start.44
  24.5 232.8 %copy-start.40 = (s32[64]{0:T(128)}, s32[64]{0:T(128)S(1)}, u32[]{:S(2)}) copy-start(s32[64]{0:T(128)S(1)} %get-tuple-element.9) | copy-start | bytes 772
  24.7 23.2 %copy-start.42 = (pred[64]{0:T(512)(128)(4,1)}, pred[64]{0:T(512)(128)(4,1)S(1)}, u32[]{:S(2)}) copy-start(pred[64]{0:T(512)(128)(4,1)S(1)} %compare_reduce_fusion) | copy-start | bytes 196
  24.7 23.2 %copy-start.37 = (s32[1024]{0:T(1024)}, s32[1024]{0:T(1024)S(1)}, u32[]{:S(2)}) copy-start(s32[1024]{0:T(1024)S(1)} %pad_clamp_fusion.4) | copy-start | bytes 12292
  24.7 23.2 %copy-start.43 = (pred[64]{0:T(512)(128)(4,1)}, pred[64]{0:T(512)(128)(4,1)S(1)}, u32[]{:S(2)}) copy-start(pred[64]{0:T(512)(128)(4,1)S(1)} %broadcast_compare_fusion.3) | copy-start | bytes 196
  51.9 11.6 %copy-start.1 = (s32[128]{0:T(128)S(1)}, s32[128]{0:T(128)}, u32[]{:S(2)}) copy-start(s32[128]{0:T(128)} %param.12) | copy-start | bytes 1540
  51.9 107.4 %all-to-all-start = ((bf16[64,128,256]{2,1,0:T(8,128)(2,1)}), bf16[64,128,256]{2,1,0:T(8,128)(2,1)}, u32[]{:S(2)}, u32[]{:S(2)}) async-start(bf16[64,128,256]{2,1,0:T(8,128)(2,1)} %select_select_fusion), calls=%async_computation.1 | async-start | bytes 8388608 | tf_op jit(solution)/shard_map/all_to_all | solution.py:97
  63.5 126.3 %copy-start.35 = (s32[16]{0:T(128)}, s32[16]{0:T(128)S(1)}, u32[]{:S(2)}) copy-start(s32[16]{0:T(128)S(1)} %get-tuple-element.24) | copy-start | bytes 196
  63.5 129.7 %copy-start.33 = (s32[16]{0:T(128)}, s32[16]{0:T(128)S(1)}, u32[]{:S(2)}) copy-start(s32[16]{0:T(128)S(1)} %get-tuple-element.25) | copy-start | bytes 196
  64.9 97.6 %copy-start.39 = (s32[1024]{0:T(1024)}, s32[1024]{0:T(1024)S(1)}, u32[]{:S(2)}) copy-start(s32[1024]{0:T(1024)S(1)} %get-tuple-element.31) | copy-start | bytes 12292
  64.9 98.6 %copy-start.38 = (s32[1024]{0:T(1024)}, s32[1024]{0:T(1024)S(1)}, u32[]{:S(2)}) copy-start(s32[1024]{0:T(1024)S(1)} %get-tuple-element.32) | copy-start | bytes 12292
  65.0 108.8 %copy-start.26 = (pred[16,128]{1,0:T(8,128)(4,1)}, pred[16,128]{1,0:T(8,128)(4,1)S(1)}, u32[]{:S(2)}) copy-start(pred[16,128]{1,0:T(8,128)(4,1)S(1)} %iota_compare_fusion) | copy-start | bytes 6148
  65.0 116.0 %copy-start.29 = (pred[16,128]{1,0:T(8,128)(4,1)}, pred[16,128]{1,0:T(8,128)(4,1)S(1)}, u32[]{:S(2)}) copy-start(pred[16,128]{1,0:T(8,128)(4,1)S(1)} %iota_compare_fusion.1) | copy-start | bytes 6148
  172.0 4.5 copy-start.22
  172.0 9.1 %copy-start.2 = (f32[16,2,128,128]{3,2,1,0:T(8,128)}, f32[16,2,128,128]{3,2,1,0:T(8,128)S(1)}, u32[]{:S(2)}) copy-start(f32[16,2,128,128]{3,2,1,0:T(8,128)S(1)} %get-tuple-element.27) | copy-start | bytes 6291460
  172.0 9.1 %copy-start.24 = (f32[16,2,128]{2,1,0:T(2,128)}, f32[16,2,128]{2,1,0:T(2,128)S(1)}, u32[]{:S(2)}) copy-start(f32[16,2,128]{2,1,0:T(2,128)S(1)} %get-tuple-element.8) | copy-start | bytes 49156
  172.0 1.8 copy-start.17
  173.8 7.3 %copy-start.20 = (f32[16,2,128]{2,1,0:T(2,128)}, f32[16,2,128]{2,1,0:T(2,128)S(1)}, u32[]{:S(2)}) copy-start(f32[16,2,128]{2,1,0:T(2,128)S(1)} %get-tuple-element.6) | copy-start | bytes 49156
  189.8 3.4 copy-start.7
  200.6 56.7 %all-to-all-start.1 = ((bf16[64,128,128]{2,1,0:T(8,128)(2,1)}), bf16[64,128,128]{2,1,0:T(8,128)(2,1)S(1)}, u32[]{:S(2)}, u32[]{:S(2)}) async-start(bf16[64,128,128]{2,1,0:T(8,128)(2,1)} %convert_element_type.42), calls=%async_computation.2 | async-start | bytes 4194304 | tf_op jit(solution)/shard_map/all_to_all | solution.py:109
  206.0 27.1 %reduce-scatter.7.cloned.1.call-start = ((), (), s32[]{:S(2)}) async-start(), calls=%async_computation.7 | async-start | bytes 327680
  262.0 14.3 %copy-start.21 = (f32[16,2,128]{2,1,0:T(2,128)S(1)}, f32[16,2,128]{2,1,0:T(2,128)}, u32[]{:S(2)}) copy-start(f32[16,2,128]{2,1,0:T(2,128)} %copy-done.20) | copy-start | bytes 49156
  262.0 56.8 %all-to-all-start.2 = ((bf16[64,128,128]{2,1,0:T(8,128)(2,1)}), bf16[64,128,128]{2,1,0:T(8,128)(2,1)S(1)}, u32[]{:S(2)}, u32[]{:S(2)}) async-start(bf16[64,128,128]{2,1,0:T(8,128)(2,1)} %select_select_fusion.1), calls=%async_computation.3 | async-start | bytes 4194304 | tf_op jit(solution)/shard_map/all_to_all | solution.py:116
  267.5 422.8 %all-reduce.5.cloned.1.call-start = ((), (), s32[]{:S(2)}) async-start(), calls=%async_computation.8 | async-start | bytes 10485760
  321.7 5.3 copy-start.3
  321.7 5.3 copy-start.25
  321.7 5.3 copy-start.30
  323.9 3.1 copy-start.12
  330.3 5.2 copy-start.23
  330.3 5.2 copy-start.27
  335.5 4.3 copy-start.4
  335.5 4.3 copy-start.28
  335.5 4.3 copy-start.31
  339.9 2.6 copy-start.10
  342.4 2.1 copy-start.11
  344.6 3.3 copy-start.18
  351.3 2.7 copy-start.13
  351.3 4.0 copy-start.6
  358.0 1.9 copy-start.8
  358.0 2.2 copy-start.9
  361.7 4.3 copy-start.36
  366.0 5.4 copy-start.34
  380.0 101.6 %copy-start.41 = (s32[64]{0:T(128)S(1)}, s32[64]{0:T(128)}, u32[]{:S(2)}) copy-start(s32[64]{0:T(128)} %copy-done.40) | copy-start | bytes 772
  481.6 12.9 %copy-start.16 = (bf16[2,128,1280]{2,1,0:T(8,128)(2,1)S(1)}, bf16[2,128,1280]{2,1,0:T(8,128)(2,1)}, u32[]{:S(2)}) copy-start(bf16[2,128,1280]{2,1,0:T(8,128)(2,1)} %param.7) | copy-start | bytes 1966084
  (4 other events, 4.5 us)
Sparse Core Ops, SparseCore 0:
  15.1 28.9 reduce-scatter.4
  210.3 22.7 reduce-scatter.6
  498.3 192.0 all-reduce.4
where the time goes:
time: 707 us; the launch traced here: 700 us
  waiting for transfers between devices  378 us (53%)
  blocking collectives  124 us (18%)
  local copies, waits for them, and re-layouts  69.1 us (10%)
  other arithmetic  43.5 us (6%)
  matrix products  39.5 us (6%)
  starting transfers between devices  31.2 us (4%)
  between operations  15.3 us (2%)
    unnamed x5, waiting for transfers between devices  200 us
    all_to_all x1, blocking collectives, on_device(): lax.all_to_all(slots.at[slot_b].add(jnp.concatenate((dkb, dvb), axis=2))....  102 us
    all_to_all x1, waiting for transfers between devices, on_device(): lax.all_to_all(outgoing_kv, 'pairs', split_axis=0, concat_axis=0, tiled=T...  94.3 us
    all_to_all x1, waiting for transfers between devices, on_device(): lax.all_to_all(outgoing_grad, 'pairs', split_axis=0, concat_axis=0, tiled...  41.3 us
    all_to_all x1, waiting for transfers between devices, on_device(): lax.all_to_all(slots.at[slot_a].add(out_a).at[slot_b].add(out_b).astype(j...  22.6 us
    unnamed x102, local copies, waits for them, and re-layouts  21.9 us
    reduce_scatter x1, waiting for transfers between devices, on_device(): lax.psum_scatter(partial_kv, 'mp', scatter_dimension=1, tiled=True)  19.3 us
  transfers between devices with their start and end apart: 6, of which 6 were waited for; matrix products, arithmetic and copies ran while one was open for 3% of the time, Pallas kernels for 0%

commit v1 on v0

v1 whole, which is shorter than its diff:
```python
import functools, math
import jax, jax.numpy as jnp
from jax import lax
from jax.sharding import PartitionSpec as P
from jax.experimental import pallas as pl
from jax.experimental.pallas import tpu as pltpu
HDIM=64
CROP=128
SCALE=HDIM**-0.5*math.log2(math.e)
NT=(((1,),(1,)),((),()))

def pair_kernel(locals_, heads, group, codes_ref, len_ref, first_ref, table_ref, hid_ref, grad_ref, list_ref, count_ref, out_acc, dk_acc, dv_acc):
    slots = codes_ref.shape[0]
    for l in range(locals_ + 1):
        count_ref[l] = 0

    def place(i, carry):
        code = codes_ref[i]
        local = jnp.where(code > 0, (code - 1) // 128, locals_)
        at = count_ref[local]
        list_ref[local, at] = jnp.maximum(code - 1, 0) % 128
        count_ref[local] = at + 1
        return carry

    lax.fori_loop(0, slots, place, 0)
    rows = lax.broadcasted_iota(jnp.int32, (CROP, CROP), 0)
    columns = lax.broadcasted_iota(jnp.int32, (1, CROP), 1)
    for l in range(locals_):
        me = first_ref[0] + l
        row_bias = jnp.where(rows < len_ref[me], 0.0, -1e30)
        count = count_ref[l]
        for extra in range(group):
            list_ref[l, count + extra] = 0
        for h in range(heads):
            own = table_ref[me * heads + h].astype(jnp.float32)
            kp = own[:HDIM].T.astype(jnp.bfloat16)
            vp = own[HDIM:2 * HDIM].T.astype(jnp.bfloat16)
            gp = own[2 * HDIM:].T.astype(jnp.bfloat16)
            out_acc[...] = jnp.zeros_like(out_acc)
            dk_acc[...] = jnp.zeros_like(dk_acc)
            dv_acc[...] = jnp.zeros_like(dv_acc)

            def step(i, carry):
                blocks, lens, live = [], [], []
                for j in range(group):
                    q = list_ref[l, i * group + j]
                    blocks.append(table_ref[q * heads + h])
                    lens.append(len_ref[q])
                    live.append(jnp.where(i * group + j < count, 1.0, 0.0))
                many = jnp.concatenate(blocks, axis=1)
                kq, vq, gq = many[:HDIM], many[HDIM:2 * HDIM], many[2 * HDIM:]
                scores = jnp.dot(kp, kq, preferred_element_type=jnp.float32)
                d_rows = jnp.dot(gp, vq, preferred_element_type=jnp.float32)
                d_cols = jnp.dot(vp, gq, preferred_element_type=jnp.float32)
                a_parts, b_parts, ds_parts = [], [], []
                for j in range(group):
                    part = slice(j * CROP, (j + 1) * CROP)
                    s = scores[:, part] * SCALE
                    sa = s + jnp.where(columns < lens[j], 0.0, -1e30)
                    ea = jnp.exp2(sa - jnp.max(sa, axis=1, keepdims=True))
                    a = ea * (live[j] / jnp.sum(ea, axis=1, keepdims=True))
                    sb = s + row_bias
                    eb = jnp.exp2(sb - jnp.max(sb, axis=0, keepdims=True))
                    b = eb * (live[j] / jnp.sum(eb, axis=0, keepdims=True))
                    da = d_rows[:, part]
                    db = d_cols[:, part]
                    ta = a * da
                    tb = b * db
                    ds = (ta - a * jnp.sum(ta, axis=1, keepdims=True)) + (tb - b * jnp.sum(tb, axis=0, keepdims=True))
                    a_parts.append(a.astype(jnp.bfloat16))
                    b_parts.append(b.astype(jnp.bfloat16))
                    ds_parts.append(ds.astype(jnp.bfloat16))
                cat = lambda x: jnp.concatenate(x, axis=1)
                out_acc[...] += lax.dot_general(cat(a_parts), vq, NT, preferred_element_type=jnp.float32)
                dv_acc[...] += lax.dot_general(cat(b_parts), gq, NT, preferred_element_type=jnp.float32)
                dk_acc[...] += lax.dot_general(cat(ds_parts), kq, NT, preferred_element_type=jnp.float32)
                return carry

            lax.fori_loop(0, (count + group - 1) // group, step, 0)
            ok = rows[:, :HDIM] < len_ref[me]
            hid_ref[l * heads + h] = jnp.where(ok, out_acc[...], 0.0).astype(jnp.bfloat16)
            grad_ref[l * heads + h] = jnp.concatenate([dk_acc[...] * HDIM ** -0.5, dv_acc[...]], axis=1).astype(jnp.bfloat16)

def pairs_call(codes, lengths, first, table, locals_, heads, group=2):
    units = locals_ * heads
    smem = pl.BlockSpec(memory_space=pltpu.SMEM)
    vmem = pl.BlockSpec(memory_space=pltpu.VMEM)
    return pl.pallas_call(
        functools.partial(pair_kernel, locals_, heads, group),
        out_shape=(jax.ShapeDtypeStruct((units, CROP, HDIM), jnp.bfloat16),
                   jax.ShapeDtypeStruct((units, CROP, 2 * HDIM), jnp.bfloat16)),
        in_specs=[smem, smem, smem, vmem],
        out_specs=(vmem, vmem),
        scratch_shapes=[pltpu.SMEM((locals_ + 1, 128 + 8), jnp.int32), pltpu.SMEM((locals_ + 1,), jnp.int32),
                        pltpu.VMEM((CROP, HDIM), jnp.float32), pltpu.VMEM((CROP, HDIM), jnp.float32), pltpu.VMEM((CROP, HDIM), jnp.float32)],
        compiler_params=pltpu.CompilerParams(vmem_limit_bytes=48 * 1024 * 1024),
    )(codes, lengths, first, table)


def on_device(embeddings, cotangent, w_qk, w_value, w_out, lengths, pair_list):
    owned, crop, width = embeddings.shape
    inner = w_qk.shape[1]
    groups = lax.axis_size("mp")
    group_cols = inner // groups
    heads = group_cols // HDIM
    rows = owned * crop
    flat = embeddings.reshape(rows, width)
    stacked = jnp.stack(
        (w_qk.reshape(width, groups, group_cols), w_value.reshape(width, groups, group_cols)),
        axis=2,
    )
    stacked = stacked.reshape(width, 2 * inner)
    partial_kv = jnp.dot(flat, stacked, preferred_element_type=jnp.float32)
    key_value = lax.psum_scatter(partial_kv, "mp", scatter_dimension=1, tiled=True).astype(jnp.bfloat16)
    me = lax.axis_index("pairs")
    workers = lax.axis_size("pairs")
    my_lengths = lax.dynamic_slice_in_dim(lengths, me * owned, owned, 0)
    rows_ok = (jnp.arange(crop, dtype=jnp.int32)[None, :] < my_lengths[:, None]).astype(jnp.float32)[:, :, None]
    partial_back = lax.dot_general(
        cotangent.reshape(rows, width), w_out, (((1,), (1,)), ((), ())), preferred_element_type=jnp.float32
    )
    head_back = (
        lax.psum_scatter(partial_back.astype(jnp.bfloat16), "mp", scatter_dimension=1, tiled=True)
        .astype(jnp.float32)
        .reshape(owned, crop, group_cols)
    )
    hidden_grad = (head_back * rows_ok).astype(jnp.bfloat16)
    both = jnp.concatenate(
        [key_value.reshape(owned, crop, 2, heads, HDIM), hidden_grad.reshape(owned, crop, 1, heads, HDIM)], axis=2
    )
    block = both.transpose(0, 3, 2, 4, 1).reshape(owned * heads, 3 * HDIM, crop)
    table = lax.all_gather(block, "pairs", axis=0, tiled=True)
    named = pair_list.reshape(workers, -1)
    partner = pair_list[:, ::-1].reshape(workers, -1)
    codes = jnp.sum(jnp.where(named // owned == me, 1 + (named % owned) * 128 + partner, 0), axis=1).astype(jnp.int32)
    hidden, grads = pairs_call(codes, lengths, (me * owned).reshape(1), table, owned, heads, 4)
    hidden = hidden.reshape(owned, heads, crop, HDIM).transpose(0, 2, 1, 3).reshape(owned, crop, group_cols)
    all_heads = lax.all_gather(hidden, "mp", axis=2, tiled=True)
    attended = jnp.dot(all_heads.reshape(rows, inner), w_out, preferred_element_type=jnp.float32)
    attended = attended.astype(jnp.bfloat16).reshape(owned, crop, width)
    grads = grads.reshape(owned, heads, crop, 2, HDIM).transpose(0, 2, 3, 1, 4).reshape(owned, crop, 2 * group_cols)
    all_grads = lax.all_gather(grads, "mp", axis=2, tiled=True).reshape(rows, 2 * inner)
    terms = lax.dot_general(all_grads, flat, (((0,), (0,)), ((), ())), preferred_element_type=jnp.float32)
    terms = terms.reshape(groups, 2, group_cols, width).transpose(1, 0, 2, 3).reshape(2, workers, inner // workers, width)
    terms = terms.transpose(1, 0, 2, 3).astype(jnp.bfloat16)
    arrived = lax.all_to_all(terms, "pairs", split_axis=0, concat_axis=0, tiled=True)
    total = jnp.sum(arrived.astype(jnp.float32), axis=0)
    return (attended, total[0].T, total[1].T)


def solution(mesh):
    in_specs = (
        P("pairs", None, "mp"),
        P("pairs", None, "mp"),
        P("mp", None),
        P("mp", None),
        P(None, "mp"),
        P(),
        P(),
    )
    out_specs = (P("pairs", None, "mp"), P("mp", "pairs"), P("mp", "pairs"))
    return jax.shard_map(on_device, mesh=mesh, in_specs=in_specs, out_specs=out_specs, check_vma=False)
```

time: 707 us -> 274 us (0.39)
  waiting for transfers between devices: 378 us -> 183 us
  blocking collectives: 124 us -> 26.1 us
  local copies, waits for them, and re-layouts: 69.1 us -> 11.8 us
  other arithmetic: 43.5 us -> 5.28 us
  matrix products: 39.5 us -> 5.67 us
  starting transfers between devices: 31.2 us -> 11.1 us
  Pallas kernels: 0 us -> 16 us
    unnamed x5 -> x4, waiting for transfers between devices: 200 us -> 18.4 us
    all_to_all x3 -> x1, waiting for transfers between devices: 158 us -> 48.6 us  [on_device(): lax.all_to_all(terms, 'pairs', split_axis=0, concat_axis=0, tiled=True)]
    all_to_all x1 -> x0, blocking collectives: 102 us -> none  [on_device(): lax.all_to_all(slots.at[slot_b].add(jnp.concatenate((dkb, dvb), axis=2))....]
    all_gather x0 -> x1, waiting for transfers between devices: none -> 88.8 us  [on_device(): table = lax.all_gather(block, 'pairs', axis=0, tiled=True)]
    dot_general x12 -> x1, matrix products: 34 us -> 0.85 us  [on_device(): lax.dot_general(all_grads, flat, (((0,), (0,)), ((), ())), preferred_elem...]
    gather x10 -> x0, local copies, waits for them, and re-layouts: 19.7 us -> none  [the longest x2 5.19 us: on_device(): grads_in[slot_b].astype(jnp.float32)]
    scatter-add x4 -> x0, other arithmetic: 16.8 us -> none  [the longest x2 6.83 us: on_device(): slots.at[slot_a].add(out_a).at[slot_b].add(out_b).astype(jnp.bfloat16)]
    pallas_call x0 -> x1, Pallas kernels: none -> 16 us  [pairs_call(): pl.pallas_call(functools.partial(pair_kernel, locals_, heads, group), out...]
  transfers between devices with their start and end apart: 6 -> 4, of which waited for: 6 -> 4; matrix products, arithmetic and copies ran while one was open for 3% -> 4% of each run, Pallas kernels for 0% -> 0%
where the time goes in v1:
time: 274 us; the launch traced here: 273 us
  waiting for transfers between devices  183 us (67%)
  blocking collectives  26.1 us (10%)
  Pallas kernels  16 us (6%)
  between operations  13.9 us (5%)
  local copies, waits for them, and re-layouts  11.8 us (4%)
  starting transfers between devices  11.1 us (4%)
  matrix products  5.67 us (2%)
  other arithmetic  5.28 us (2%)
    all_gather x1, waiting for transfers between devices, on_device(): table = lax.all_gather(block, 'pairs', axis=0, tiled=True)  88.8 us
    all_to_all x1, waiting for transfers between devices, on_device(): lax.all_to_all(terms, 'pairs', split_axis=0, concat_axis=0, tiled=True)  48.6 us
    reduce_scatter x1, waiting for transfers between devices, on_device(): lax.psum_scatter(partial_kv, 'mp', scatter_dimension=1, tiled=True)  27.4 us
    unnamed x4, waiting for transfers between devices  18.4 us
    pallas_call x1, Pallas kernels, pairs_call(): pl.pallas_call(functools.partial(pair_kernel, locals_, heads, group), out...  16 us
    all_gather x1, blocking collectives, on_device(): lax.all_gather(grads, 'mp', axis=2, tiled=True).reshape(rows, 2 * inner)  13.8 us
    all_gather x1, blocking collectives, on_device(): all_heads = lax.all_gather(hidden, 'mp', axis=2, tiled=True)  12.3 us
    all_to_all x1, starting transfers between devices, on_device(): lax.all_to_all(terms, 'pairs', split_axis=0, concat_axis=0, tiled=True)  11 us
  transfers between devices with their start and end apart: 4, of which 4 were waited for; matrix products, arithmetic and copies ran while one was open for 4% of the time, Pallas kernels for 0%

profile of v1, /device:TPU:6, one launch (start us, length us, event | category | flops | bytes accessed | tf_op | source)
XLA Modules:
  0.0 273.0 jit_solution(9024800835816922655)
XLA Ops:
  7.2 0.0 copy-start
  7.2 0.0 reduce-scatter.7.cloned.1.call-start
  7.2 1.3 copy-done
  8.5 1.6 convolution_convert_fusion.2
  10.1 0.8 copy.46
  11.0 0.0 reduce-scatter.7.cloned.1.call-update
  11.0 0.0 reduce-scatter.5.cloned.1.call-start
  11.0 1.6 copy.33
  12.6 2.4 copy.34
  15.1 1.6 pad_maximum_fusion
  16.7 0.0 copy-done.2
  16.7 0.0 copy-start.1
  16.7 1.9 convolution_bitcast_fusion
  18.6 0.0 reduce-scatter.5.cloned.1.call-update
  18.6 0.0 all-gather.2.cloned.1.call-start
  18.7 0.0 copy-done.1
  18.7 0.1 dynamic_slice.3
  18.8 0.1 compare_convert_fusion
  18.8 18.4 %reduce-scatter.7.cloned.1.call-done = bf16[128,256]{1,0:T(8,128)(2,1)} async-done(((bf16[512,256]{1,0:T(8,128)(2,1)}), bf16[128,256]{1,0:T(8,128)(2,1)}) %reduce-scatter.7.cloned.1.call-update) | async-done | bytes 65552
  37.2 0.9 copy.47
  38.1 0.1 copy.35
  38.3 0.1 reshape.110
  38.4 27.4 %reduce-scatter.5.cloned.1.call-done = f32[256,256]{0,1:T(8,128)} async-done(((f32[256,1024]{0,1:T(8,128)}), f32[256,256]{0,1:T(8,128)}) %reduce-scatter.5.cloned.1.call-update) | async-done | bytes 262160 | tf_op jit(solution)/shard_map/reduce_scatter | solution.py:114
  65.8 1.0 convert_element_type.42
  66.8 0.3 maximum_bitcast_fusion
  67.0 0.7 copy.36
  67.8 0.0 all-gather.2.cloned.1.call-update
  67.8 0.2 rev.3
  68.0 0.1 fusion.2
  68.1 0.1 reduce_sum.26
  68.2 0.1 reduce_sum.27.codes_ref
  68.3 88.8 %all-gather.2.cloned.1.call-done.table_ref = bf16[256,192,128]{2,1,0:T(8,128)(2,1)} async-done(((bf16[4,192,128]{2,1,0:T(8,128)(2,1)}), bf16[256,192,128]{2,1,0:T(8,128)(2,1)}) %all-gather.2.cloned.1.call-update) | async-done | bytes 12582928 | tf_op jit(solution)/shard_map/all_gather | solution.py:132
  157.0 16.0 %shard_map.94 = (bf16[4,128,64]{2,1,0:T(8,128)(2,1)S(1)}, bf16[4,128,128]{2,1,0:T(8,128)(2,1)S(1)}) custom-call(s32[64]{0:T(128)S(1)} %reduce_sum.27.codes_ref, s32[128]{0:T(128)S(1)} %copy-done.1, s32[1]{0:T(128)} %bitcast.first_ref, bf16[256,192,128]{2,1,0:T(8,128)(2,1)} %all-gather.2.cloned.1.call-done.table_ref), custom_call_target="tpu_custom_call" | custom-call | tf_op jit(solution)/shard_map/pallas_call | solution.py:88
  173.1 0.1 copy.39
  173.2 13.8 %all_gather.11 = bf16[2,128,1024]{1,2,0:T(8,128)(2,1)S(1)} all-gather(bf16[2,128,256]{1,2,0:T(8,128)(2,1)S(1)} %bitcast.69), channel_id=1, replica_groups=mesh['pairs'=64,'mp'=4] {'mp'}, dimensions={2}, use_global_device_ids=true | all-gather | bytes 655360 | tf_op jit(solution)/shard_map/all_gather | solution.py:142
  187.0 0.2 copy.41
  187.2 0.2 copy.42
  187.5 0.8 fusion
  188.3 0.2 copy.43
  188.5 1.7 copy.44
  190.2 11.0 %all-to-all-start = ((bf16[64,2,8,1280]{3,2,1,0:T(8,128)(2,1)}), bf16[64,2,8,1280]{3,2,1,0:T(8,128)(2,1)}, u32[]{:S(2)}, u32[]{:S(2)}) async-start(bf16[64,2,8,1280]{3,2,1,0:T(8,128)(2,1)} %copy.44), calls=%async_computation.1 | async-start | bytes 5242880 | tf_op jit(solution)/shard_map/all_to_all | solution.py:146
  201.2 0.1 copy.37
  201.3 12.3 %all_gather.10 = bf16[2,128,512]{1,2,0:T(8,128)(2,1)S(1)} all-gather(bf16[2,128,128]{1,2,0:T(8,128)(2,1)S(1)} %bitcast.71), channel_id=1, replica_groups=mesh['pairs'=64,'mp'=4] {'mp'}, dimensions={2}, use_global_device_ids=true | all-gather | bytes 327680 | tf_op jit(solution)/shard_map/all_gather | solution.py:138
  213.6 0.1 copy.38
  213.7 1.3 convolution_convert_fusion.1
  215.1 48.6 %all-to-all-done = bf16[64,2,8,1280]{3,2,1,0:T(8,128)(2,1)} async-done(((bf16[64,2,8,1280]{3,2,1,0:T(8,128)(2,1)}), bf16[64,2,8,1280]{3,2,1,0:T(8,128)(2,1)}, u32[]{:S(2)}, u32[]{:S(2)}) %all-to-all-start) | async-done | bytes 2621472 | tf_op jit(solution)/shard_map/all_to_all | solution.py:146
  263.7 2.1 convert_reduce_fusion
  265.8 0.6 slice_bitcast_fusion
  (6 shorter events, 0.1 us)
Async XLA Ops:
  7.2 1.3 copy-start
  7.2 30.0 %reduce-scatter.7.cloned.1.call-start = ((), (), s32[]{:S(2)}) async-start(), calls=%async_computation.5 | async-start | bytes 327680
  11.0 54.8 %reduce-scatter.5.cloned.1.call-start = ((), (), s32[]{:S(2)}) async-start(), calls=%async_computation.3 | async-start | bytes 1310720 | tf_op jit(solution)/shard_map/reduce_scatter | solution.py:114
  15.1 1.6 copy-start.2
  16.7 1.9 copy-start.1
  18.6 49.2 %copy-start.3 = (s32[1024,2]{0,1:T(2,128)S(1)}, s32[1024,2]{0,1:T(2,128)}, u32[]{:S(2)}) copy-start(s32[1024,2]{0,1:T(2,128)} %param.13) | copy-start | bytes 24580
  18.6 138.4 %all-gather.2.cloned.1.call-start = ((), (), s32[]{:S(2)}) async-start(), calls=%async_computation.4 | async-start | bytes 12779520 | tf_op jit(solution)/shard_map/all_gather | solution.py:132
  190.2 73.5 %all-to-all-start = ((bf16[64,2,8,1280]{3,2,1,0:T(8,128)(2,1)}), bf16[64,2,8,1280]{3,2,1,0:T(8,128)(2,1)}, u32[]{:S(2)}, u32[]{:S(2)}) async-start(bf16[64,2,8,1280]{3,2,1,0:T(8,128)(2,1)} %copy.44), calls=%async_computation.1 | async-start | bytes 5242880 | tf_op jit(solution)/shard_map/all_to_all | solution.py:146
Sparse Core Ops, SparseCore 0:
  11.1 26.0 reduce-scatter.6
  39.9 25.8 reduce-scatter.4
  69.1 87.8 all-gather.1

commit v2 on v1

v2 whole, which is shorter than its diff:
```python
import functools
import math

import jax
import jax.numpy as jnp
from jax import lax
from jax.experimental import pallas as pl
from jax.experimental.pallas import tpu as pltpu
from jax.sharding import PartitionSpec as P

HDIM = 64
CROP = 128
SCALE = HDIM**-0.5 * math.log2(math.e)
NT = (((1,), (1,)), ((), ()))
NZ, NX, NY = 8, 4, 4
CHIPS = NZ * NX
LOCALS = 4
GROUP = 4
MESH = pl.DeviceIdType.MESH
VMEM_LIMIT = 56 * 1024 * 1024


def place():
    me = lax.axis_index("pairs")
    chip = me // 2
    return chip // NX, chip % NX, me % 2, lax.axis_index("mp")


def device(z, x, c, y):
    return ((z * NX + x) * 2 + c, y)


def remote(src, dst, send, recv, to):
    return pltpu.make_async_remote_copy(
        src_ref=src, dst_ref=dst, send_sem=send, recv_sem=recv, device_id=to, device_id_type=MESH
    )


def greet(others):
    barrier = pltpu.get_barrier_semaphore()
    for other in others:
        pl.semaphore_signal(barrier, inc=1, device_id=other, device_id_type=MESH)
    pl.semaphore_wait(barrier, len(others))


def swap_halves(value):
    return pltpu.roll(value, HDIM, 1)


def gather_kernel(
    len_ref, emb_ref, cot_ref, wq_ref, wv_ref, wo_ref, table_ref, sib_ref,
    kv_send, kv_recv, g_send, g_recv, block, kv_ssem, kv_rsem, g_ssem, g_rsem, ssem, rsem, lsem,
):
    z, x, c, y = place()
    chip = z * NX + x
    mine = y * 2 + c
    column = [device(z, x, cd, (y + d) % NY) for d in (1, 2, 3) for cd in (0, 1)]
    sibling = device(z, x, 1 - c, y)
    up, down = (z + 1) % NZ, (z + NZ - 1) % NZ
    east, west = (x + 1) % NX, (x + NX - 1) % NX
    ring = [device(up, x, c, y), device(down, x, c, y), device(z, east, c, y), device(z, west, c, y)]
    greet(column + [sibling] + ring)

    share = remote(emb_ref, sib_ref, lsem.at[1], lsem.at[2], sibling)
    share.start()

    low = lax.broadcasted_iota(jnp.int32, (2 * CROP, 2 * HDIM), 1) < HDIM

    def pieces(yd):
        at = pl.ds(pl.multiple_of(yd * 2 * HDIM, 2 * HDIM), 2 * HDIM)
        k = jnp.dot(emb_ref[...], wq_ref[:, at], preferred_element_type=jnp.float32)
        v = jnp.dot(emb_ref[...], wv_ref[:, at], preferred_element_type=jnp.float32)
        g = lax.dot_general(cot_ref[...], wo_ref[at, :], NT, preferred_element_type=jnp.float32)
        first, second = g[:CROP], g[CROP:]
        half = low[:CROP]
        kv = (jnp.where(low, k, swap_halves(v)), jnp.where(low, swap_halves(k), v))
        gg = (
            jnp.where(half, first, swap_halves(second)).astype(jnp.bfloat16),
            jnp.where(half, swap_halves(first), second).astype(jnp.bfloat16),
        )
        return kv, gg

    def kv_copy(slot, to):
        return remote(kv_send.at[slot], kv_recv.at[mine], kv_ssem.at[slot], kv_rsem.at[mine], to)

    def g_copy(slot, to):
        return remote(g_send.at[slot], g_recv.at[mine], g_ssem.at[slot], g_rsem.at[mine], to)

    def away(step, carry):
        d = jnp.where(step == 0, 2, jnp.where(step == 1, 1, 3))
        yd = (y + d) % NY
        kv, gg = pieces(yd)
        for cd in (0, 1):
            slot = yd * 2 + cd
            kv_send[slot] = kv[cd]
            g_send[slot] = gg[cd]
            kv_copy(slot, device(z, x, cd, yd)).start()
            g_copy(slot, device(z, x, cd, yd)).start()
        return carry

    lax.fori_loop(0, 3, away, 0)
    kv, gg = pieces(y)
    other = y * 2 + 1 - c
    kv_send[other] = jnp.where(c == 0, kv[1], kv[0])
    g_send[other] = jnp.where(c == 0, gg[1], gg[0])
    kv_copy(other, sibling).start()
    g_copy(other, sibling).start()
    kv_recv[mine] = jnp.where(c == 0, kv[0], kv[1])
    g_recv[mine] = jnp.where(c == 0, gg[0], gg[1])

    def arrive(step, carry):
        slot = (mine + step) % (2 * NY)
        remote(kv_send.at[slot], kv_recv.at[slot], kv_ssem.at[slot], kv_rsem.at[slot], sibling).wait_recv()
        remote(g_send.at[slot], g_recv.at[slot], g_ssem.at[slot], g_rsem.at[slot], sibling).wait_recv()
        return carry

    lax.fori_loop(1, 2 * NY, arrive, 0)
    lanes = lax.broadcasted_iota(jnp.int32, (HDIM, CROP), 1)
    for cs in (0, 1):
        kv_sum = (kv_recv[cs] + kv_recv[2 + cs]) + (kv_recv[4 + cs] + kv_recv[6 + cs])
        g_sum = (g_recv[cs].astype(jnp.float32) + g_recv[2 + cs].astype(jnp.float32)) + (
            g_recv[4 + cs].astype(jnp.float32) + g_recv[6 + cs].astype(jnp.float32)
        )
        g_turned = g_sum.T
        for j in (0, 1):
            p = cs * 2 + j
            block[p, : 2 * HDIM] = kv_sum[j * CROP : (j + 1) * CROP].T.astype(jnp.bfloat16)
            ok = lanes < len_ref[chip * LOCALS + p]
            block[p, 2 * HDIM :] = jnp.where(ok, g_turned[j * HDIM : (j + 1) * HDIM], 0.0).astype(jnp.bfloat16)

    keep = pltpu.make_async_copy(block, table_ref.at[pl.ds(chip * LOCALS, LOCALS)], lsem.at[0])
    keep.start()
    sent = []

    def part(bz, bx, half):
        at = (bz * NX + bx) * LOCALS
        if half is None:
            return table_ref.at[pl.ds(at, LOCALS)]
        return table_ref.at[pl.ds(at + half * (LOCALS // 2), LOCALS // 2)]

    def push(bz, bx, half, to, own=False):
        sem = rsem.at[bz * NX + bx, half or 0]
        src = block if own else part(bz, bx, half)
        copy = remote(src, part(bz, bx, half), ssem.at[len(sent)], sem, device(to[0], to[1], c, y))
        copy.start()
        sent.append(copy)

    def landed(bz, bx, half=None):
        ref = part(bz, bx, half)
        remote(ref, ref, ssem.at[0], rsem.at[bz * NX + bx, half or 0], device(up, x, c, y)).wait_recv()

    def cross(bz):
        landed(bz, west)
        push(bz, west, 0, (z, east))
        landed(bz, east)
        push(bz, east, 1, (z, west))

    @pl.when(c == 0)
    def _():
        sent.clear()
        for to in ((z, east), (z, west), (up, x), (down, x)):
            push(z, x, None, to, own=True)
        ready = [z]
        for s in range(1, NZ // 2 + 1):
            lo, hi = (z + NZ - s) % NZ, (z + s) % NZ
            fresh = [lo, hi]
            if s < NZ // 2:
                for bz, to, half in ((lo, up, 0), (hi, down, 1)):
                    landed(bz, x)
                    push(bz, x, None if s < NZ // 2 - 1 else half, (to, x))
                    push(bz, x, None, (z, east))
                    push(bz, x, None, (z, west))
            else:
                fresh = [lo]
                landed(lo, x, 0)
                landed(lo, x, 1)
                push(lo, x, None, (z, east))
                push(lo, x, None, (z, west))
            for bz in ready:
                cross(bz)
            ready = fresh
        for bz in ready:
            cross(bz)
        for bz in range(NZ):
            landed(bz, (x + 2) % NX, 0)
            landed(bz, (x + 2) % NX, 1)
        for copy in sent:
            copy.wait_send()

    @pl.when(c == 1)
    def _():
        sent.clear()
        for to in ((up, x), (down, x), (z, east), (z, west)):
            push(z, x, None, to, own=True)
        for bx, to, half in ((west, east, 0), (east, west, 1)):
            landed(z, bx)
            push(z, bx, half, (z, to))
            push(z, bx, None, (up, x))
            push(z, bx, None, (down, x))
        far = (x + 2) % NX
        landed(z, far, 0)
        landed(z, far, 1)
        push(z, far, None, (up, x))
        push(z, far, None, (down, x))
        for s in range(1, NZ // 2 + 1):
            lo, hi = (z + NZ - s) % NZ, (z + s) % NZ
            for bx in (x, west, east, far):
                if s < NZ // 2:
                    last = s == NZ // 2 - 1
                    landed(lo, bx)
                    push(lo, bx, 0 if last else None, (up, x))
                    landed(hi, bx)
                    push(hi, bx, 1 if last else None, (down, x))
                else:
                    landed(lo, bx, 0)
                    landed(lo, bx, 1)
        for copy in sent:
            copy.wait_send()

    def leave(step, carry):
        slot = (mine + step) % (2 * NY)
        kv_copy(slot, sibling).wait_send()
        g_copy(slot, sibling).wait_send()
        return carry

    lax.fori_loop(1, 2 * NY, leave, 0)
    keep.wait()
    share.wait()


def gather_call(lengths, emb, cot, w_qk, w_value, w_out):
    rows, width = emb.shape
    smem = pl.BlockSpec(memory_space=pltpu.SMEM)
    vmem = pl.BlockSpec(memory_space=pltpu.VMEM)
    hbm = pl.BlockSpec(memory_space=pl.ANY)
    dma = pltpu.SemaphoreType.DMA
    return pl.pallas_call(
        gather_kernel,
        out_shape=(
            jax.ShapeDtypeStruct((CHIPS * LOCALS, 3 * HDIM, CROP), jnp.bfloat16),
            jax.ShapeDtypeStruct((rows, width), jnp.bfloat16),
        ),
        in_specs=[smem] + [vmem] * 5,
        out_specs=(hbm, hbm),
        scratch_shapes=[
            pltpu.VMEM((2 * NY, rows, 2 * HDIM), jnp.float32),
            pltpu.VMEM((2 * NY, rows, 2 * HDIM), jnp.float32),
            pltpu.VMEM((2 * NY, CROP, 2 * HDIM), jnp.bfloat16),
            pltpu.VMEM((2 * NY, CROP, 2 * HDIM), jnp.bfloat16),
            pltpu.VMEM((LOCALS, 3 * HDIM, CROP), jnp.bfloat16),
            dma((2 * NY,)),
            dma((2 * NY,)),
            dma((2 * NY,)),
            dma((2 * NY,)),
            dma((48,)),
            dma((CHIPS, 2)),
            dma((3,)),
        ],
        compiler_params=pltpu.CompilerParams(
            collective_id=0, has_side_effects=True, vmem_limit_bytes=VMEM_LIMIT
        ),
    )(lengths, emb, cot, w_qk, w_value, w_out)


def pair_kernel(codes_ref, len_ref, first_ref, table_ref, hid_ref, grad_ref, list_ref, count_ref, out_acc, dk_acc, dv_acc):
    for l in range(LOCALS + 1):
        count_ref[l] = 0

    def sort(i, carry):
        code = codes_ref[i]
        local = jnp.where(code > 0, (code - 1) // CROP, LOCALS)
        at = count_ref[local]
        list_ref[local, at] = jnp.maximum(code - 1, 0) % CROP
        count_ref[local] = at + 1
        return carry

    lax.fori_loop(0, codes_ref.shape[0], sort, 0)
    rows = lax.broadcasted_iota(jnp.int32, (CROP, CROP), 0)
    columns = lax.broadcasted_iota(jnp.int32, (1, CROP), 1)
    for l in range(LOCALS):
        me = first_ref[0] + l
        row_bias = jnp.where(rows < len_ref[me], 0.0, -1e30)
        count = count_ref[l]
        for extra in range(GROUP):
            list_ref[l, count + extra] = 0
        own = table_ref[me].astype(jnp.float32)
        kp = own[:HDIM].T.astype(jnp.bfloat16)
        vp = own[HDIM : 2 * HDIM].T.astype(jnp.bfloat16)
        gp = own[2 * HDIM :].T.astype(jnp.bfloat16)
        out_acc[...] = jnp.zeros_like(out_acc)
        dk_acc[...] = jnp.zeros_like(dk_acc)
        dv_acc[...] = jnp.zeros_like(dv_acc)

        def step(i, carry):
            blocks, lens, live = [], [], []
            for j in range(GROUP):
                q = list_ref[l, i * GROUP + j]
                blocks.append(table_ref[q])
                lens.append(len_ref[q])
                live.append(jnp.where(i * GROUP + j < count, 1.0, 0.0))
            many = jnp.concatenate(blocks, axis=1)
            kq, vq, gq = many[:HDIM], many[HDIM : 2 * HDIM], many[2 * HDIM :]
            scores = jnp.dot(kp, kq, preferred_element_type=jnp.float32)
            d_rows = jnp.dot(gp, vq, preferred_element_type=jnp.float32)
            d_cols = jnp.dot(vp, gq, preferred_element_type=jnp.float32)
            a_parts, b_parts, ds_parts = [], [], []
            for j in range(GROUP):
                part = slice(j * CROP, (j + 1) * CROP)
                s = scores[:, part] * SCALE
                sa = s + jnp.where(columns < lens[j], 0.0, -1e30)
                ea = jnp.exp2(sa - jnp.max(sa, axis=1, keepdims=True))
                a = ea * (live[j] / jnp.sum(ea, axis=1, keepdims=True))
                sb = s + row_bias
                eb = jnp.exp2(sb - jnp.max(sb, axis=0, keepdims=True))
                b = eb * (live[j] / jnp.sum(eb, axis=0, keepdims=True))
                ta = a * d_rows[:, part]
                tb = b * d_cols[:, part]
                ds = (ta - a * jnp.sum(ta, axis=1, keepdims=True)) + (
                    tb - b * jnp.sum(tb, axis=0, keepdims=True)
                )
                a_parts.append(a.astype(jnp.bfloat16))
                b_parts.append(b.astype(jnp.bfloat16))
                ds_parts.append(ds.astype(jnp.bfloat16))
            for acc, parts, other in ((out_acc, a_parts, vq), (dv_acc, b_parts, gq), (dk_acc, ds_parts, kq)):
                acc[...] += lax.dot_general(
                    jnp.concatenate(parts, axis=1), other, NT, preferred_element_type=jnp.float32
                )
            return carry

        lax.fori_loop(0, (count + GROUP - 1) // GROUP, step, 0)
        ok = rows[:, :HDIM] < len_ref[me]
        hid_ref[l // 2, :, (l % 2) * HDIM : (l % 2 + 1) * HDIM] = jnp.where(ok, out_acc[...], 0.0).astype(
            jnp.bfloat16
        )
        turned = jnp.concatenate([dk_acc[...] * HDIM**-0.5, dv_acc[...]], axis=1).T
        for core in range(2):
            eights = []
            for xd in range(NX):
                at = (xd * 2 + core) * 8
                eights += [turned[at : at + 8], turned[HDIM + at : HDIM + at + 8]]
            grad_ref[core, :, l * CROP : (l + 1) * CROP] = jnp.concatenate(eights, axis=0).astype(jnp.bfloat16)


def pair_call(codes, lengths, first, table):
    smem = pl.BlockSpec(memory_space=pltpu.SMEM)
    vmem = pl.BlockSpec(memory_space=pltpu.VMEM)
    return pl.pallas_call(
        pair_kernel,
        out_shape=(
            jax.ShapeDtypeStruct((2, CROP, 2 * HDIM), jnp.bfloat16),
            jax.ShapeDtypeStruct((2, HDIM, LOCALS * CROP), jnp.bfloat16),
        ),
        in_specs=[smem, smem, smem, vmem],
        out_specs=(vmem, vmem),
        scratch_shapes=[
            pltpu.SMEM((LOCALS + 1, 2 * CROP), jnp.int32),
            pltpu.SMEM((LOCALS + 1,), jnp.int32),
            pltpu.VMEM((CROP, HDIM), jnp.float32),
            pltpu.VMEM((CROP, HDIM), jnp.float32),
            pltpu.VMEM((CROP, HDIM), jnp.float32),
        ],
        compiler_params=pltpu.CompilerParams(vmem_limit_bytes=VMEM_LIMIT),
    )(codes, lengths, first, table)


def ring_sum(n, term, plus, minus, send, recv, ssem, rsem, between=None):
    steps = n // 2
    half = send.shape[-1] // 2
    sent = []
    for s in range(steps):
        d = steps - s
        for way, to in ((0, plus), (1, minus)):
            value = term(d if way == 0 else n - d)
            spot = slice(way * half, (way + 1) * half) if s == 0 else slice(None)
            if s == 0:
                send[way, s, :, spot] = value[:, spot].astype(jnp.bfloat16)
            else:
                back = slice(way * half, (way + 1) * half) if s == 1 else slice(None)
                landing = recv.at[way, s - 1, :, back]
                remote(landing, landing, ssem.at[way, s - 1], rsem.at[way, s - 1], to).wait_recv()
                if s == 1:
                    send[way, s] = value.astype(jnp.bfloat16)
                    send[way, s, :, back] = (value[:, back] + recv[way, 0, :, back].astype(jnp.float32)).astype(
                        jnp.bfloat16
                    )
                else:
                    send[way, s] = (value + recv[way, s - 1].astype(jnp.float32)).astype(jnp.bfloat16)
            copy = remote(
                send.at[way, s, :, spot], recv.at[way, s, :, spot], ssem.at[way, s], rsem.at[way, s], to
            )
            copy.start()
            sent.append(copy)
        if s == 0 and between is not None:
            between()
    total = term(0)
    for way, to in ((0, plus), (1, minus)):
        landing = recv.at[way, steps - 1]
        remote(landing, landing, ssem.at[way, steps - 1], rsem.at[way, steps - 1], to).wait_recv()
        total = total + recv[way, steps - 1].astype(jnp.float32)
    for copy in sent:
        copy.wait_send()
    return total


def finish_kernel(
    hid_ref, grad_ref, emb_ref, sib_ref, wo_ref, att_ref, sum_ref,
    hid_recv, g_recv, terms, hidden, z0_send, z0_recv, x0_send, x0_recv, x1_send, x1_recv, z1_send, z1_recv, held,
    h_ssem, h_rsem, g_ssem, g_rsem, zs_sem, zr_sem, xs_sem, xr_sem,
):
    z, x, c, y = place()
    mine = y * 2 + c
    column = [(cd, d) for d in (2, 1, 3) for cd in (0, 1)]
    sibling = device(z, x, 1 - c, y)
    up, down = device((z + 1) % NZ, x, c, y), device((z + NZ - 1) % NZ, x, c, y)
    east, west = device(z, (x + 1) % NX, c, y), device(z, (x + NX - 1) % NX, c, y)
    greet([device(z, x, cd, (y + d) % NY) for cd, d in column] + [sibling, up, down, east, west])

    def copies(cd, yd):
        slot = yd * 2 + cd
        to = device(z, x, cd, yd)
        return (
            remote(grad_ref.at[cd], g_recv.at[mine], g_ssem.at[slot], g_rsem.at[mine], to),
            remote(hid_ref.at[cd], hid_recv.at[mine], h_ssem.at[slot], h_rsem.at[mine], to),
        )

    outgoing = [copies(cd, (y + d) % NY) for cd, d in column] + [copies(1 - c, y)]
    for kind in (0, 1):
        for copy in outgoing:
            copy[kind].start()
    g_recv[mine] = grad_ref[c]
    hid_recv[mine] = hid_ref[c]

    def arrive_g(step, carry):
        slot = (mine + step) % (2 * NY)
        remote(g_recv.at[slot], g_recv.at[slot], g_ssem.at[slot], g_rsem.at[slot], sibling).wait_recv()
        return carry

    lax.fori_loop(1, 2 * NY, arrive_g, 0)
    spots = 2 * NY * HDIM
    all_g = g_recv[...].reshape(spots, 4 * CROP)
    own = jnp.where(c == 0, all_g[:, : 2 * CROP], all_g[:, 2 * CROP :])
    theirs = jnp.where(c == 0, all_g[:, 2 * CROP :], all_g[:, : 2 * CROP])
    terms[...] = (
        jnp.dot(own, emb_ref[...], preferred_element_type=jnp.float32)
        + jnp.dot(theirs, sib_ref[...], preferred_element_type=jnp.float32)
    ).reshape(terms.shape)

    def attend():
        def arrive_h(step, carry):
            slot = (mine + step) % (2 * NY)
            remote(hid_recv.at[slot], hid_recv.at[slot], h_ssem.at[slot], h_rsem.at[slot], sibling).wait_recv()
            return carry

        lax.fori_loop(1, 2 * NY, arrive_h, 0)
        low = lax.broadcasted_iota(jnp.int32, (CROP, 2 * HDIM), 1) < HDIM
        for yy in range(NY):
            even = hid_recv[2 * yy].astype(jnp.float32)
            odd = hid_recv[2 * yy + 1].astype(jnp.float32)
            at = slice(yy * 2 * HDIM, (yy + 1) * 2 * HDIM)
            hidden[:CROP, at] = jnp.where(low, even, swap_halves(odd)).astype(jnp.bfloat16)
            hidden[CROP:, at] = jnp.where(low, swap_halves(even), odd).astype(jnp.bfloat16)
        att_ref[...] = jnp.dot(hidden[...], wo_ref[...], preferred_element_type=jnp.float32).astype(jnp.bfloat16)

    @pl.when(c == 0)
    def _():
        line = ring_sum(
            NZ,
            lambda d: terms[(z + d) % NZ].reshape(HDIM, terms.shape[-1]),
            up, down, z0_send, z0_recv, zs_sem, zr_sem, attend,
        )
        held[...] = line.reshape(held.shape)
        sum_ref[...] = ring_sum(
            NX, lambda d: held[(x + d) % NX], east, west, x0_send, x0_recv, xs_sem, xr_sem
        )

    @pl.when(c == 1)
    def _():
        plane = ring_sum(
            NX,
            lambda d: terms[:, (x + d) % NX].reshape(NZ * 16, terms.shape[-1]),
            east, west, x1_send, x1_recv, xs_sem, xr_sem, attend,
        )
        terms[:, 0] = plane.reshape(NZ, 16, terms.shape[-1])
        sum_ref[...] = ring_sum(
            NZ, lambda d: terms[(z + d) % NZ, 0], up, down, z1_send, z1_recv, zs_sem, zr_sem
        )

    for pair in outgoing:
        for copy in pair:
            copy.wait_send()


def finish_call(hid, grads, emb, sib, w_out):
    rows, width = emb.shape
    vmem = pl.BlockSpec(memory_space=pltpu.VMEM)
    dma = pltpu.SemaphoreType.DMA
    bf = jnp.bfloat16
    return pl.pallas_call(
        finish_kernel,
        out_shape=(
            jax.ShapeDtypeStruct((rows, width), bf),
            jax.ShapeDtypeStruct((16, width), jnp.float32),
        ),
        in_specs=[vmem] * 5,
        out_specs=(vmem, vmem),
        scratch_shapes=[
            pltpu.VMEM((2 * NY, CROP, 2 * HDIM), bf),
            pltpu.VMEM((2 * NY, HDIM, 4 * CROP), bf),
            pltpu.VMEM((NZ, NX, 16, width), jnp.float32),
            pltpu.VMEM((2 * CROP, 2 * NY * HDIM), bf),
            pltpu.VMEM((2, NZ // 2, HDIM, width), bf),
            pltpu.VMEM((2, NZ // 2, HDIM, width), bf),
            pltpu.VMEM((2, NX // 2, 16, width), bf),
            pltpu.VMEM((2, NX // 2, 16, width), bf),
            pltpu.VMEM((2, NX // 2, NZ * 16, width), bf),
            pltpu.VMEM((2, NX // 2, NZ * 16, width), bf),
            pltpu.VMEM((2, NZ // 2, 16, width), bf),
            pltpu.VMEM((2, NZ // 2, 16, width), bf),
            pltpu.VMEM((NX, 16, width), jnp.float32),
            dma((2 * NY,)),
            dma((2 * NY,)),
            dma((2 * NY,)),
            dma((2 * NY,)),
            dma((2, NZ // 2)),
            dma((2, NZ // 2)),
            dma((2, NX // 2)),
            dma((2, NX // 2)),
        ],
        compiler_params=pltpu.CompilerParams(
            collective_id=1, has_side_effects=True, vmem_limit_bytes=VMEM_LIMIT
        ),
    )(hid, grads, emb, sib, w_out)


def on_device(embeddings, cotangent, w_qk, w_value, w_out, lengths, pair_list):
    owned, crop, width = embeddings.shape
    rows = owned * crop
    emb = embeddings.reshape(rows, width)
    chip = lax.axis_index("pairs") // 2
    named = pair_list.reshape(lax.axis_size("pairs"), -1)
    partner = pair_list[:, ::-1].reshape(named.shape)
    owner = 2 * chip + jnp.arange(2, dtype=jnp.int32)[:, None, None]
    codes = jnp.where(named[None] // owned == owner, 1 + (named[None] - 4 * chip) * CROP + partner[None], 0)
    codes = jnp.sum(codes, axis=2).astype(jnp.int32).reshape(-1)
    table, sib = gather_call(lengths, emb, cotangent.reshape(rows, width), w_qk, w_value, w_out)
    hid, grads = pair_call(codes, lengths, (LOCALS * chip).reshape(1), table)
    attended, sums = finish_call(hid, grads, emb, sib, w_out)
    return (attended.reshape(embeddings.shape), sums[:8].T, sums[8:].T)


def solution(mesh):
    in_specs = (
        P("pairs", None, "mp"),
        P("pairs", None, "mp"),
        P("mp", None),
        P("mp", None),
        P(None, "mp"),
        P(),
        P(),
    )
    out_specs = (P("pairs", None, "mp"), P("mp", "pairs"), P("mp", "pairs"))
    return jax.shard_map(on_device, mesh=mesh, in_specs=in_specs, out_specs=out_specs, check_vma=False)
```

time: 274 us -> 132 us (0.48)
  waiting for transfers between devices: 183 us -> 0 us
  Pallas kernels: 16 us -> 121 us
  blocking collectives: 26.1 us -> 0 us
  between operations: 13.9 us -> 0.7 us
  starting transfers between devices: 11.1 us -> 0 us
  matrix products: 5.67 us -> 0 us
  other arithmetic: 5.28 us -> 0.13 us
  local copies, waits for them, and re-layouts: 11.8 us -> 8.6 us
    pallas_call x1 -> x3, Pallas kernels: 16 us -> 121 us  [the longest x1 59.8 us: gather_call(): pl.pallas_call(gather_kernel, out_shape=(jax.ShapeDtypeStruct((CHIPS * LO...]
    all_gather x1 -> x0, waiting for transfers between devices: 88.8 us -> none  [on_device(): table = lax.all_gather(block, 'pairs', axis=0, tiled=True)]
    all_to_all x1 -> x0, waiting for transfers between devices: 48.6 us -> none  [on_device(): lax.all_to_all(terms, 'pairs', split_axis=0, concat_axis=0, tiled=True)]
    reduce_scatter x1 -> x0, waiting for transfers between devices: 27.4 us -> none  [on_device(): lax.psum_scatter(partial_kv, 'mp', scatter_dimension=1, tiled=True)]
    all_gather x2 -> x0, blocking collectives: 26.1 us -> none  [the longest x1 13.8 us: on_device(): lax.all_gather(grads, 'mp', axis=2, tiled=True).reshape(rows, 2 * inner)]
    unnamed x4 -> x0, waiting for transfers between devices: 18.4 us -> none
    all_to_all x1 -> x0, starting transfers between devices: 11 us -> none  [on_device(): lax.all_to_all(terms, 'pairs', split_axis=0, concat_axis=0, tiled=True)]
    dot_general x4 -> x0, matrix products: 5.67 us -> none  [the longest x1 1.85 us: on_device(): partial_kv = jnp.dot(flat, stacked, preferred_element_type=jnp.float32)]
  transfers between devices with their start and end apart: 4 -> 0, of which waited for: 4 -> 0; matrix products, arithmetic and copies ran while one was open for 4% -> 0% of each run, Pallas kernels for 0% -> 0%
where the time goes in v2:
time: 132 us; the launch traced here: 131 us
  Pallas kernels  121 us (92%)
  local copies, waits for them, and re-layouts  8.6 us (7%)
    pallas_call x1, Pallas kernels, gather_call(): pl.pallas_call(gather_kernel, out_shape=(jax.ShapeDtypeStruct((CHIPS * LO...  59.8 us
    pallas_call x1, Pallas kernels, finish_call(): pl.pallas_call(finish_kernel, out_shape=(jax.ShapeDtypeStruct((rows, widt...  44.8 us
    pallas_call x1, Pallas kernels, pair_call(): pl.pallas_call(pair_kernel, out_shape=(jax.ShapeDtypeStruct((2, CROP, 2 *...  16.8 us
    rev x2, local copies, waits for them, and re-layouts, on_device(): partner = pair_list[:, ::-1].reshape(named.shape)  3.05 us
    unnamed x2, local copies, waits for them, and re-layouts  2.88 us

profile of v2, /device:TPU:6, one launch (start us, length us, event | category | flops | bytes accessed | tf_op | source)
XLA Modules:
  0.0 130.9 jit_solution(2008192972824475093)
XLA Ops:
  0.7 2.8 %rev.3 = s32[1024,2]{0,1:T(2,128)S(1)} reverse(s32[1024,2]{0,1:T(2,128)} %param.13), dimensions={1} | reverse | bytes 16384 | tf_op jit(solution)/shard_map/rev | solution.py:541
  3.5 0.2 copy.14
  3.7 0.3 broadcast_in_dim_reshape.8
  4.0 0.9 copy.12
  4.9 0.3 broadcast_in_dim_reshape.7
  5.2 0.1 copy.13
  5.2 0.1 copy.15
  5.3 0.1 select_reduce_fusion
  5.4 0.6 reshape.103.codes_ref
  6.0 59.8 %shard_map.94 = (bf16[128,192,128]{2,1,0:T(8,128)(2,1)}, bf16[256,1280]{1,0:T(8,128)(2,1)}) custom-call(s32[128]{0:T(128)} %len_ref.3, bf16[256,1280]{1,0:T(8,128)(2,1)} %bitcast.8, bf16[256,1280]{1,0:T(8,128)(2,1)} %bitcast.11, bf16[1280,512]{1,0:T(8,128)(2,1)} %wq_ref.1, bf16[1280,512]{1,0:T(8,128)(2,1)} %wv_ref.1, bf16[512,1280]{1,0:T(8,128)(2,1)} %wo_ref.3), custom_call_target="tpu_custom_call" | custom-call | tf_op jit(solution)/shard_map/pallas_call | solution.py:237
  65.8 16.8 %shard_map.95 = (bf16[2,128,128]{2,1,0:T(8,128)(2,1)}, bf16[2,64,512]{2,1,0:T(8,128)(2,1)}) custom-call(s32[128]{0:T(128)} %reshape.103.codes_ref, s32[128]{0:T(128)} %len_ref.3, s32[1]{0:T(128)} %bitcast.first_ref, bf16[128,192,128]{2,1,0:T(8,128)(2,1)} %get-tuple-element.9.table_ref), custom_call_target="tpu_custom_call" | custom-call | tf_op jit(solution)/shard_map/pallas_call | solution.py:347
  82.6 44.8 %shard_map.96 = (bf16[256,1280]{1,0:T(8,128)(2,1)}, f32[16,1280]{1,0:T(8,128)}) custom-call(bf16[2,128,128]{2,1,0:T(8,128)(2,1)} %get-tuple-element.10.hid_ref, bf16[2,64,512]{2,1,0:T(8,128)(2,1)} %get-tuple-element.11.grad_ref, bf16[256,1280]{1,0:T(8,128)(2,1)} %bitcast.9, bf16[256,1280]{1,0:T(8,128)(2,1)} %get-tuple-element.12.sib_ref, ...), custom_call_target="tpu_custom_call" | custom-call | tf_op jit(solution)/shard_map/pallas_call | solution.py:498
  127.5 1.4 %slice_bitcast_fusion = (f32[1280,8]{0,1:T(8,128)}, f32[1280,8]{0,1:T(8,128)}) fusion(f32[16,1280]{1,0:T(8,128)} %get-tuple-element.14), kind=kLoop, calls=%fused_computation.4 | loop fusion | bytes 163840 | tf_op jit(solution)/shard_map/transpose | solution.py:548
  128.9 2.0 %copy.17 = bf16[2,128,1280]{2,1,0:T(8,128)(2,1)} copy(bf16[2,128,1280]{2,1,0:T(8,128)(2,1)} %bitcast.10) | data formatting | bytes 1310720
  (2 shorter events, 0.0 us)

commit v3 on v1

v3 whole, which is shorter than its diff:
```python
import math

import jax
import jax.numpy as jnp
from jax import lax
from jax.experimental import pallas as pl
from jax.experimental.pallas import tpu as pltpu
from jax.sharding import PartitionSpec as P

HDIM = 64
CROP = 128
SCALE = HDIM**-0.5 * math.log2(math.e)
NT = (((1,), (1,)), ((), ()))
NZ, NX, NY = 8, 4, 4
CHIPS = NZ * NX
LOCALS = 4
HEADS = 2 * NY
MESH = pl.DeviceIdType.MESH
VMEM_LIMIT = 56 * 1024 * 1024


def place():
    me = lax.axis_index("pairs")
    chip = me // 2
    return chip // NX, chip % NX, me % 2, lax.axis_index("mp")


def device(z, x, c, y):
    return ((z * NX + x) * 2 + c, y)


def column_of(x, c):
    return jnp.where(c == x // 2, x, NX - 1 - x)


def mate_of(x):
    return x + 1 - 2 * (x % 2)


def remote(src, dst, send, recv, to):
    return pltpu.make_async_remote_copy(
        src_ref=src, dst_ref=dst, send_sem=send, recv_sem=recv, device_id=to, device_id_type=MESH
    )


def greet(others):
    barrier = pltpu.get_barrier_semaphore()
    for other in others:
        pl.semaphore_signal(barrier, inc=1, device_id=other, device_id_type=MESH)
    pl.semaphore_wait(barrier, len(others))


def gather_kernel(
    len_ref, pairs_ref, emb_hbm, cot_hbm, wq_hbm, wv_hbm, wo_hbm, table_ref, sib_ref, codes_ref,
    emb, cot, wq, wv, wo, k_send, k_recv, vg_send, vg_recv, block, seed,
    lsem, k_ssem, k_rsem, vg_ssem, vg_rsem, bsem, ssem, rsem,
):
    z, x, c, y = place()
    mine = y * 2 + c
    sibling = device(z, x, 1 - c, y)
    partner = device(z, NX - 1 - x, 1 - c, y)
    mate = device(z, mate_of(x), c, y)
    up, down = device((z + 1) % NZ, x, c, y), device((z + NZ - 1) % NZ, x, c, y)
    col, mate_col = column_of(x, c), column_of(mate_of(x), c)
    sib_col, sib_mate_col = column_of(x, 1 - c), column_of(mate_of(x), 1 - c)
    kept = c == x // 2

    loads = [
        pltpu.make_async_copy(src, dst, lsem.at[i])
        for i, (src, dst) in enumerate(
            ((emb_hbm, emb), (wq_hbm, wq), (wv_hbm, wv), (cot_hbm, cot), (wo_hbm, wo))
        )
    ]
    for load in loads:
        load.start()
    greet(
        [device(z, x, cd, (y + d) % NY) for d in (1, 2, 3) for cd in (0, 1)] + [sibling, partner, mate, up, down]
    )
    for load in loads:
        load.wait()
    share = remote(emb, sib_ref, lsem.at[5], lsem.at[6], sibling)
    share.start()

    def copies(j, slot, to):
        return (
            remote(k_send.at[j, slot], k_recv.at[j, mine], k_ssem.at[j, slot], k_rsem.at[j, mine], to),
            remote(vg_send.at[j, slot], vg_recv.at[j, mine], vg_ssem.at[j, slot], vg_rsem.at[j, mine], to),
        )

    def project(j):
        rows = slice(j * CROP, (j + 1) * CROP)

        def pieces(yd):
            at = pl.ds(pl.multiple_of(yd * 2 * HDIM, 2 * HDIM), 2 * HDIM)
            k = jnp.dot(emb[rows], wq[:, at], preferred_element_type=jnp.float32).T
            v = jnp.dot(emb[rows], wv[:, at], preferred_element_type=jnp.float32).T.astype(jnp.bfloat16)
            g = lax.dot_general(cot[rows], wo[at, :], NT, preferred_element_type=jnp.float32).T.astype(jnp.bfloat16)
            return [
                (k[cd * HDIM : (cd + 1) * HDIM], v[cd * HDIM : (cd + 1) * HDIM], g[cd * HDIM : (cd + 1) * HDIM])
                for cd in (0, 1)
            ]

        def away(step, carry):
            d = jnp.where(step == 0, 2, jnp.where(step == 1, 1, 3))
            yd = (y + d) % NY
            for cd, (k, v, g) in enumerate(pieces(yd)):
                slot = yd * 2 + cd
                k_send[j, slot] = k
                vg_send[j, slot, :HDIM] = v
                vg_send[j, slot, HDIM:] = g
                for copy in copies(j, slot, device(z, x, cd, yd)):
                    copy.start()
            return carry

        lax.fori_loop(0, 3, away, 0)
        both = pieces(y)
        other = y * 2 + 1 - c
        k_send[j, other] = jnp.where(c == 0, both[1][0], both[0][0])
        vg_send[j, other, :HDIM] = jnp.where(c == 0, both[1][1], both[0][1])
        vg_send[j, other, HDIM:] = jnp.where(c == 0, both[1][2], both[0][2])
        for copy in copies(j, other, sibling):
            copy.start()
        k_recv[j, mine] = jnp.where(c == 0, both[0][0], both[1][0])
        vg_recv[j, mine, :HDIM] = jnp.where(c == 0, both[0][1], both[1][1])
        vg_recv[j, mine, HDIM:] = jnp.where(c == 0, both[0][2], both[1][2])

    def settle(j):
        def arrive(step, carry):
            slot = (mine + step) % HEADS
            for copy in (
                remote(k_recv.at[j, slot], k_recv.at[j, slot], k_ssem.at[j, slot], k_rsem.at[j, slot], sibling),
                remote(vg_recv.at[j, slot], vg_recv.at[j, slot], vg_ssem.at[j, slot], vg_rsem.at[j, slot], sibling),
            ):
                copy.wait_recv()
            return carry

        lax.fori_loop(1, HEADS, arrive, 0)
        lanes = lax.broadcasted_iota(jnp.int32, (HDIM, CROP), 1)

        def fill(ref):
            for cs in (0, 1):
                k = (k_recv[j, cs] + k_recv[j, 2 + cs]) + (k_recv[j, 4 + cs] + k_recv[j, 6 + cs])
                vg = [vg_recv[j, 2 * yy + cs].astype(jnp.float32) for yy in range(NY)]
                vg = (vg[0] + vg[1]) + (vg[2] + vg[3])
                ok = lanes < len_ref[(z * NX + x) * LOCALS + 2 * cs + j]
                ref[j, cs, :HDIM] = k.astype(jnp.bfloat16)
                ref[j, cs, HDIM : 2 * HDIM] = vg[:HDIM].astype(jnp.bfloat16)
                ref[j, cs, 2 * HDIM :] = jnp.where(ok, vg[HDIM:], 0.0).astype(jnp.bfloat16)

        @pl.when(kept)
        def _():
            fill(seed)

        @pl.when(jnp.logical_not(kept))
        def _():
            fill(block)
            swap = remote(block.at[j], seed.at[j], bsem.at[0, j], bsem.at[1, j], partner)
            swap.start()
            swap.wait_recv()

        pltpu.make_async_copy(seed.at[j], part(j, z, col), bsem.at[2, j]).start()

    def part(j, bz, bx, half=None):
        at = j * 2 * CHIPS + (bz * NX + bx) * 2
        return table_ref.at[pl.ds(at, 2)] if half is None else table_ref.at[pl.ds(at + half, 1)]

    def landed(j, bz, bx, half=None):
        ref = part(j, bz, bx, half)
        remote(ref, ref, ssem.at[0], rsem.at[j, bz * NX + bx, half or 0], sibling).wait_recv()

    def spread(j, sent, first):
        def push(bz, bx, to, half=None, src=None):
            dst = part(j, bz, bx, half)
            sem = rsem.at[j, bz * NX + bx, half or 0]
            copy = remote(dst if src is None else src, dst, ssem.at[len(sent)], sem, to)
            copy.start()
            sent.append(copy)

        def hop(s, bx, extra):
            for bz, to, half in (((z + NZ - s) % NZ, up, 0), ((z + s) % NZ, down, 1)):
                landed(j, bz, bx)
                push(bz, bx, to, half if s == NZ // 2 - 1 else None)
                for other in extra:
                    push(bz, bx, other)

        def meet(bx, extra):
            bz = (z + NZ // 2) % NZ
            landed(j, bz, bx, 0)
            landed(j, bz, bx, 1)
            for other in extra:
                push(bz, bx, other)

        def relay(bz):
            landed(j, bz, mate_col)
            push(bz, mate_col, sibling)

        if first == "z":
            for to in (up, down, mate, sibling):
                push(z, col, to, src=seed.at[j])
            ready = [z]
            yield
            for s in range(1, NZ // 2):
                hop(s, col, (mate, sibling))
                for bz in ready:
                    relay(bz)
                ready = [(z + NZ - s) % NZ, (z + s) % NZ]
                yield
            meet(col, (mate, sibling))
            for bz in ready:
                relay(bz)
            yield
            relay((z + NZ // 2) % NZ)
            yield
        else:
            for to in (mate, up, down, sibling):
                push(z, col, to, src=seed.at[j])
            yield
            landed(j, z, mate_col)
            for to in (up, down, sibling):
                push(z, mate_col, to)
            yield
            for s in range(1, NZ // 2):
                for bx in (col, mate_col):
                    hop(s, bx, (sibling,))
                yield
            for bx in (col, mate_col):
                meet(bx, (sibling,))
            yield

    def whole(first):
        sent = []
        now, later = spread(0, sent, first), spread(1, sent, first)
        next(now)
        project(1)
        next(now)
        next(now)
        settle(1)
        live = [later, now]
        while live:
            for one in list(live):
                if next(one, 1) == 1:
                    live.remove(one)
        for j in (0, 1):
            for bz in range(NZ):
                landed(j, bz, sib_col)
                landed(j, bz, sib_mate_col)
        for copy in sent:
            copy.wait_send()

    project(0)
    first = (z * NX + col) * LOCALS
    a, b = pairs_ref[0:1], pairs_ref[1:2]
    owners = lax.broadcasted_iota(jnp.int32, (8, 1), 0) + first // 2
    codes = jnp.where(a // 2 == owners, 1 + (a - first) * CROP + b, 0) + jnp.where(
        b // 2 == owners, 1 + (b - first) * CROP + a, 0
    )
    count = pairs_ref.shape[1]
    each = count // (2 * CHIPS)
    segment = (
        lax.broadcasted_iota(jnp.int32, (count, CROP), 0) // each
        == lax.broadcasted_iota(jnp.int32, (count, CROP), 1)
    ).astype(jnp.float32)
    codes_ref[...] = jnp.dot(
        codes.astype(jnp.float32), segment, precision=lax.Precision.HIGHEST, preferred_element_type=jnp.float32
    ).astype(jnp.int32)
    settle(0)

    @pl.when(c == 0)
    def _():
        whole("z")

    @pl.when(c == 1)
    def _():
        whole("x")

    for j in (0, 1):

        def leave(step, carry):
            for copy in copies(j, (mine + step) % HEADS, sibling):
                copy.wait_send()
            return carry

        lax.fori_loop(1, HEADS, leave, 0)
        pltpu.make_async_copy(seed.at[j], part(j, z, col), bsem.at[2, j]).wait()

        @pl.when(jnp.logical_not(kept))
        def _():
            remote(block.at[j], seed.at[j], bsem.at[0, j], bsem.at[1, j], partner).wait_send()

    share.wait()


def gather_call(lengths, pairs, emb, cot, w_qk, w_value, w_out):
    rows, width = emb.shape
    smem = pl.BlockSpec(memory_space=pltpu.SMEM)
    vmem = pl.BlockSpec(memory_space=pltpu.VMEM)
    hbm = pl.BlockSpec(memory_space=pl.ANY)
    dma = pltpu.SemaphoreType.DMA
    bf = jnp.bfloat16
    return pl.pallas_call(
        gather_kernel,
        out_shape=(
            jax.ShapeDtypeStruct((CHIPS * LOCALS, 3 * HDIM, CROP), bf),
            jax.ShapeDtypeStruct((rows, width), bf),
            jax.ShapeDtypeStruct((8, CROP), jnp.int32),
        ),
        in_specs=[smem, vmem] + [hbm] * 5,
        out_specs=(hbm, hbm, vmem),
        scratch_shapes=[pltpu.VMEM(v.shape, bf) for v in (emb, cot, w_qk, w_value, w_out)]
        + [
            pltpu.VMEM((2, HEADS, HDIM, CROP), jnp.float32),
            pltpu.VMEM((2, HEADS, HDIM, CROP), jnp.float32),
            pltpu.VMEM((2, HEADS, 2 * HDIM, CROP), bf),
            pltpu.VMEM((2, HEADS, 2 * HDIM, CROP), bf),
            pltpu.VMEM((2, 2, 3 * HDIM, CROP), bf),
            pltpu.VMEM((2, 2, 3 * HDIM, CROP), bf),
            dma((7,)),
            dma((2, HEADS)),
            dma((2, HEADS)),
            dma((2, HEADS)),
            dma((2, HEADS)),
            dma((3, 2)),
            dma((72,)),
            dma((2, CHIPS, 2)),
        ],
        compiler_params=pltpu.CompilerParams(
            collective_id=0, has_side_effects=True, vmem_limit_bytes=VMEM_LIMIT
        ),
    )(lengths, pairs, emb, cot, w_qk, w_value, w_out)


def pair_kernel(
    codes_ref, len_ref, first_ref, table_hbm, hid_ref, grad_ref, table_ref, list_ref, count_ref, out_acc, dk_acc, dv_acc, sem
):
    load = pltpu.make_async_copy(table_hbm, table_ref, sem.at[0])
    load.start()
    for l in range(LOCALS + 1):
        count_ref[l] = 0

    def sort(i, carry):
        for o in (0, 1):
            code = codes_ref[o, i]
            local = jnp.where(code > 0, (code - 1) // CROP, LOCALS)
            at = count_ref[local]
            list_ref[local, at] = jnp.maximum(code - 1, 0) % CROP
            count_ref[local] = at + 1
        return carry

    lax.fori_loop(0, 2 * CHIPS, sort, 0)
    rows = lax.broadcasted_iota(jnp.int32, (CROP, CROP), 0)
    columns = lax.broadcasted_iota(jnp.int32, (1, CROP), 1)
    load.wait()

    def spot(p):
        return (p % 2) * 2 * CHIPS + p // 2

    for l in range(LOCALS):
        me = first_ref[0] + l
        row_bias = jnp.where(rows < len_ref[me], 0.0, -1e30)
        count = count_ref[l]
        for extra in range(8):
            list_ref[l, count + extra] = 0
        own = table_ref[spot(me)].astype(jnp.float32)
        kp = own[:HDIM].T.astype(jnp.bfloat16)
        vp = own[HDIM : 2 * HDIM].T.astype(jnp.bfloat16)
        gp = own[2 * HDIM :].T.astype(jnp.bfloat16)
        out_acc[...] = jnp.zeros_like(out_acc)
        dk_acc[...] = jnp.zeros_like(dk_acc)
        dv_acc[...] = jnp.zeros_like(dv_acc)

        def step(base, group):
            blocks, lens, live = [], [], []
            for j in range(group):
                q = list_ref[l, base + j]
                blocks.append(table_ref[spot(q)])
                lens.append(len_ref[q])
                live.append(jnp.where(base + j < count, 1.0, 0.0))
            many = jnp.concatenate(blocks, axis=1)
            kq, vq, gq = many[:HDIM], many[HDIM : 2 * HDIM], many[2 * HDIM :]
            scores = jnp.dot(kp, kq, preferred_element_type=jnp.float32)
            d_rows = jnp.dot(gp, vq, preferred_element_type=jnp.float32)
            d_cols = jnp.dot(vp, gq, preferred_element_type=jnp.float32)
            a_parts, b_parts, ds_parts = [], [], []
            for j in range(group):
                part = slice(j * CROP, (j + 1) * CROP)
                s = scores[:, part] * SCALE
                sa = s + jnp.where(columns < lens[j], 0.0, -1e30)
                ea = jnp.exp2(sa - jnp.max(sa, axis=1, keepdims=True))
                a = ea * (live[j] / jnp.sum(ea, axis=1, keepdims=True))
                sb = s + row_bias
                eb = jnp.exp2(sb - jnp.max(sb, axis=0, keepdims=True))
                b = eb * (live[j] / jnp.sum(eb, axis=0, keepdims=True))
                ta = a * d_rows[:, part]
                tb = b * d_cols[:, part]
                ds = (ta - a * jnp.sum(ta, axis=1, keepdims=True)) + (
                    tb - b * jnp.sum(tb, axis=0, keepdims=True)
                )
                a_parts.append(a.astype(jnp.bfloat16))
                b_parts.append(b.astype(jnp.bfloat16))
                ds_parts.append(ds.astype(jnp.bfloat16))
            for acc, parts, other in ((out_acc, a_parts, vq), (dv_acc, b_parts, gq), (dk_acc, ds_parts, kq)):
                acc[...] += lax.dot_general(
                    jnp.concatenate(parts, axis=1), other, NT, preferred_element_type=jnp.float32
                )

        def eight(i, carry):
            step(i * 8, 8)
            return carry

        def four(i, carry):
            step(big * 8, 4)
            return carry

        big = (count + 3) // 8
        lax.fori_loop(0, big, eight, 0)
        lax.fori_loop(0, jnp.where(count > big * 8, 1, 0), four, 0)
        ok = rows[:, :HDIM] < len_ref[me]
        hid_ref[l // 2, :, (l % 2) * HDIM : (l % 2 + 1) * HDIM] = jnp.where(ok, out_acc[...], 0.0).astype(
            jnp.bfloat16
        )
        turned = jnp.concatenate([dk_acc[...] * HDIM**-0.5, dv_acc[...]], axis=1).T
        for core in range(2):
            eights = []
            for xd in range(NX):
                at = (xd * 2 + core) * 8
                eights += [turned[at : at + 8], turned[HDIM + at : HDIM + at + 8]]
            grad_ref[core, :, l * CROP : (l + 1) * CROP] = jnp.concatenate(eights, axis=0).astype(jnp.bfloat16)


def pair_call(codes, lengths, first, table):
    smem = pl.BlockSpec(memory_space=pltpu.SMEM)
    vmem = pl.BlockSpec(memory_space=pltpu.VMEM)
    hbm = pl.BlockSpec(memory_space=pl.ANY)
    return pl.pallas_call(
        pair_kernel,
        out_shape=(
            jax.ShapeDtypeStruct((2, CROP, 2 * HDIM), jnp.bfloat16),
            jax.ShapeDtypeStruct((2, HDIM, LOCALS * CROP), jnp.bfloat16),
        ),
        in_specs=[smem, smem, smem, hbm],
        out_specs=(vmem, vmem),
        scratch_shapes=[
            pltpu.VMEM(table.shape, jnp.bfloat16),
            pltpu.SMEM((LOCALS + 1, 2 * CROP), jnp.int32),
            pltpu.SMEM((LOCALS + 1,), jnp.int32),
            pltpu.VMEM((CROP, HDIM), jnp.float32),
            pltpu.VMEM((CROP, HDIM), jnp.float32),
            pltpu.VMEM((CROP, HDIM), jnp.float32),
            pltpu.SemaphoreType.DMA((1,)),
        ],
        compiler_params=pltpu.CompilerParams(vmem_limit_bytes=VMEM_LIMIT),
    )(codes, lengths, first, table)


def ring_sum(n, term, plus, minus, send, recv, ssem, rsem, done):
    steps = n // 2
    half = send.shape[-1] // 2
    sent = []
    for s in range(steps):
        d = steps - s
        for way, to in ((0, plus), (1, minus)):
            own = slice(way * half, (way + 1) * half)
            rest = slice((1 - way) * half, (2 - way) * half)
            value = term(d if way == 0 else n - d)
            if s > 0:
                landing = recv.at[way, s - 1, :, own] if s == 1 else recv.at[way, s - 1]
                remote(landing, landing, ssem.at[way, s - 1], rsem.at[way, s - 1], to).wait_recv()
            send[way, s, :, own] = (
                value[:, own] if s == 0 else value[:, own] + recv[way, s - 1, :, own].astype(jnp.float32)
            ).astype(jnp.bfloat16)
            if s == 1:
                send[way, s, :, rest] = value[:, rest].astype(jnp.bfloat16)
            elif s > 1:
                send[way, s, :, rest] = (
                    value[:, rest] + recv[way, s - 1, :, rest].astype(jnp.float32)
                ).astype(jnp.bfloat16)
            spot = own if s == 0 else slice(None)
            copy = remote(
                send.at[way, s, :, spot], recv.at[way, s, :, spot], ssem.at[way, s], rsem.at[way, s], to
            )
            copy.start()
            sent.append(copy)
        yield
    total = term(0)
    for way, to in ((0, plus), (1, minus)):
        landing = recv.at[way, steps - 1]
        remote(landing, landing, ssem.at[way, steps - 1], rsem.at[way, steps - 1], to).wait_recv()
        total = total + recv[way, steps - 1].astype(jnp.float32)
    done(total)
    for copy in sent:
        copy.wait_send()
    yield


def together(*rings):
    live = list(rings)
    while live:
        for one in list(live):
            if next(one, 1) == 1:
                live.remove(one)


def finish_kernel(
    hid_ref, grad_ref, emb_hbm, sib_hbm, hidden_ref, qk_ref, value_ref,
    emb, sib, hid_recv, g_recv, terms, z_send, z_recv, x_send, x_recv, line, last_send, last_recv,
    lsem, h_ssem, h_rsem, g_ssem, g_rsem, zs_sem, zr_sem, xs_sem, xr_sem, ls_sem, lr_sem,
):
    z, x, c, y = place()
    col = column_of(x, c)
    kept = c == x // 2
    mine = 2 * y + x // 2
    loads = [pltpu.make_async_copy(emb_hbm, emb, lsem.at[0]), pltpu.make_async_copy(sib_hbm, sib, lsem.at[1])]
    for load in loads:
        load.start()
    sibling = device(z, x, 1 - c, y)
    up, down = device((z + 1) % NZ, x, c, y), device((z + NZ - 1) % NZ, x, c, y)
    east, west = device(z, (x + 1) % NX, c, y), device(z, (x + NX - 1) % NX, c, y)
    near = [device(z, x, cd, (y + d) % NY) for d in (1, 2, 3) for cd in (0, 1)] + [sibling]
    near += [device(z, NX - 1 - x, cd, (y + d) % NY) for d in range(NY) for cd in (0, 1)]
    near += [device(z, (x + d) % NX, c, y) for d in range(1, NX)]
    near += [device((z + d) % NZ, x, c, y) for d in range(1, NZ)]
    greet(near)

    ways = [(d, cd) for d in (2, 1, 3, 0) for cd in (0, 1)]

    def outgoing(d, cd, kind):
        yd = (y + d) % NY
        slot = yd * 2 + cd
        to = device(z, col, cd, yd)
        if kind == 0:
            return remote(grad_ref.at[cd], g_recv.at[mine], g_ssem.at[slot], g_rsem.at[mine], to)
        return remote(hid_ref.at[cd], hid_recv.at[mine], h_ssem.at[slot], h_rsem.at[mine], to)

    def away(d, cd):
        return jnp.logical_not(kept & (cd == c)) if d == 0 else None

    for kind in (0, 1):
        for d, cd in ways:
            if d:
                outgoing(d, cd, kind).start()
            else:

                @pl.when(away(d, cd))
                def _():
                    outgoing(d, cd, kind).start()

    @pl.when(kept)
    def _():
        g_recv[mine] = grad_ref[c]
        hid_recv[mine] = hid_ref[c]

    def arrive(ref, ss, rs):
        def one(slot, carry):
            @pl.when(jnp.logical_not(kept & (slot == mine)))
            def _():
                remote(ref.at[slot], ref.at[slot], ss.at[slot], rs.at[slot], sibling).wait_recv()

            return carry

        lax.fori_loop(0, HEADS, one, 0)

    for load in loads:
        load.wait()
    arrive(g_recv, g_ssem, g_rsem)
    width = emb.shape[-1]
    all_g = g_recv[...].reshape(HEADS * HDIM, LOCALS * CROP)
    own = jnp.where(c == 0, all_g[:, : 2 * CROP], all_g[:, 2 * CROP :])
    theirs = jnp.where(c == 0, all_g[:, 2 * CROP :], all_g[:, : 2 * CROP])
    terms[...] = (
        jnp.dot(own, emb[...], preferred_element_type=jnp.float32)
        + jnp.dot(theirs, sib[...], preferred_element_type=jnp.float32)
    ).reshape(terms.shape)

    def finish(n, term, to):
        sends = []
        for d in sorted(range(1, n), key=lambda d: -min(d, n - d)):
            last_send[d] = term(d).astype(jnp.bfloat16)
            copy = remote(last_send.at[d], last_recv.at[d], ls_sem.at[d], lr_sem.at[d], to(d))
            copy.start()
            sends.append(copy)
        total = term(0)
        for copy in sends:
            copy.wait_recv()
        for d in range(1, n):
            total = total + last_recv[d].astype(jnp.float32)
        qk_ref[...] = total[:8]
        value_ref[...] = total[8:]
        for copy in sends:
            copy.wait_send()

    def heads():
        arrive(hid_recv, h_ssem, h_rsem)
        low = lax.broadcasted_iota(jnp.int32, (CROP, 2 * HDIM), 1) < HDIM
        for yy in range(NY):
            even = hid_recv[2 * yy].astype(jnp.float32)
            odd = hid_recv[2 * yy + 1].astype(jnp.float32)
            at = slice(yy * 2 * HDIM, (yy + 1) * 2 * HDIM)
            hidden_ref[:CROP, at] = jnp.where(low, even, pltpu.roll(odd, HDIM, 1)).astype(jnp.bfloat16)
            hidden_ref[CROP:, at] = jnp.where(low, pltpu.roll(even, HDIM, 1), odd).astype(jnp.bfloat16)

    @pl.when(c == 0)
    def _():
        def ring(i):
            def done(total):
                line[2 * i : 2 * i + 2] = total.reshape(2, 16, width)

            return ring_sum(
                NZ,
                lambda d: terms[(z + d) % NZ, 2 * i : 2 * i + 2].reshape(32, width),
                up, down, z_send.at[i], z_recv.at[i], zs_sem.at[i], zr_sem.at[i], done,
            )

        together(ring(0), ring(1))
        finish(NX, lambda d: line[(x + d) % NX], lambda d: device(z, (x + d) % NX, c, y))

    @pl.when(c == 1)
    def _():
        def ring(i):
            def done(total):
                line[4 * i : 4 * i + 4] = total.reshape(4, 16, width)

            return ring_sum(
                NX,
                lambda d: terms[4 * i : 4 * i + 4, (x + d) % NX].reshape(64, width),
                east, west, x_send.at[i], x_recv.at[i], xs_sem.at[i], xr_sem.at[i], done,
            )

        together(ring(0), ring(1))
        finish(NZ, lambda d: line[(z + d) % NZ], lambda d: device((z + d) % NZ, x, c, y))

    heads()
    for d, cd in ways:
        for kind in (0, 1):
            if d:
                outgoing(d, cd, kind).wait_send()
            else:

                @pl.when(away(d, cd))
                def _():
                    outgoing(d, cd, kind).wait_send()


def finish_call(hid, grads, emb, sib):
    rows, width = emb.shape
    vmem = pl.BlockSpec(memory_space=pltpu.VMEM)
    hbm = pl.BlockSpec(memory_space=pl.ANY)
    dma = pltpu.SemaphoreType.DMA
    bf = jnp.bfloat16
    return pl.pallas_call(
        finish_kernel,
        out_shape=(
            jax.ShapeDtypeStruct((rows, HEADS * HDIM), bf),
            jax.ShapeDtypeStruct((8, width), jnp.float32),
            jax.ShapeDtypeStruct((8, width), jnp.float32),
        ),
        in_specs=[vmem, vmem, hbm, hbm],
        out_specs=(vmem, vmem, vmem),
        scratch_shapes=[
            pltpu.VMEM((rows, width), bf),
            pltpu.VMEM((rows, width), bf),
            pltpu.VMEM((HEADS, CROP, 2 * HDIM), bf),
            pltpu.VMEM((HEADS, HDIM, LOCALS * CROP), bf),
            pltpu.VMEM((NZ, NX, 16, width), jnp.float32),
            pltpu.VMEM((2, 2, NZ // 2, 32, width), bf),
            pltpu.VMEM((2, 2, NZ // 2, 32, width), bf),
            pltpu.VMEM((2, 2, NX // 2, 64, width), bf),
            pltpu.VMEM((2, 2, NX // 2, 64, width), bf),
            pltpu.VMEM((NZ, 16, width), jnp.float32),
            pltpu.VMEM((NZ, 16, width), bf),
            pltpu.VMEM((NZ, 16, width), bf),
            dma((2,)),
            dma((HEADS,)),
            dma((HEADS,)),
            dma((HEADS,)),
            dma((HEADS,)),
            dma((2, 2, NZ // 2)),
            dma((2, 2, NZ // 2)),
            dma((2, 2, NX // 2)),
            dma((2, 2, NX // 2)),
            dma((NZ,)),
            dma((NZ,)),
        ],
        compiler_params=pltpu.CompilerParams(
            collective_id=1, has_side_effects=True, vmem_limit_bytes=VMEM_LIMIT
        ),
    )(hid, grads, emb, sib)


def on_device(embeddings, cotangent, w_qk, w_value, w_out, lengths, pair_list):
    owned, crop, width = embeddings.shape
    rows = owned * crop
    emb = embeddings.reshape(rows, width)
    z, x, c, _ = place()
    first = LOCALS * (z * NX + column_of(x, c))
    table, sib, codes = gather_call(
        lengths, pair_list.T, emb, cotangent.reshape(rows, width), w_qk, w_value, w_out
    )
    hid, grads = pair_call(codes, lengths, first.reshape(1), table)
    hidden, grad_qk, grad_value = finish_call(hid, grads, emb, sib)
    attended = jnp.dot(hidden, w_out, preferred_element_type=jnp.float32).astype(jnp.bfloat16)
    return (attended.reshape(embeddings.shape), grad_qk.T, grad_value.T)


def solution(mesh):
    in_specs = (
        P("pairs", None, "mp"),
        P("pairs", None, "mp"),
        P("mp", None),
        P("mp", None),
        P(None, "mp"),
        P(),
        P(),
    )
    out_specs = (P("pairs", None, "mp"), P("mp", "pairs"), P("mp", "pairs"))
    return jax.shard_map(on_device, mesh=mesh, in_specs=in_specs, out_specs=out_specs, check_vma=False)
```

time: 274 us -> 116 us (0.42)
  waiting for transfers between devices: 183 us -> 0 us
  Pallas kernels: 16 us -> 111 us
  blocking collectives: 26.1 us -> 0 us
  between operations: 13.9 us -> 0.76 us
  starting transfers between devices: 11.1 us -> 0 us
  local copies, waits for them, and re-layouts: 11.8 us -> 1.25 us
  other arithmetic: 5.28 us -> 0 us
  matrix products: 5.67 us -> 2.3 us
    pallas_call x1 -> x3, Pallas kernels: 16 us -> 111 us  [the longest x1 58.9 us: gather_call(): pl.pallas_call(gather_kernel, out_shape=(jax.ShapeDtypeStruct((CHIPS * LO...]
    all_gather x1 -> x0, waiting for transfers between devices: 88.8 us -> none  [on_device(): table = lax.all_gather(block, 'pairs', axis=0, tiled=True)]
    all_to_all x1 -> x0, waiting for transfers between devices: 48.6 us -> none  [on_device(): lax.all_to_all(terms, 'pairs', split_axis=0, concat_axis=0, tiled=True)]
    reduce_scatter x1 -> x0, waiting for transfers between devices: 27.4 us -> none  [on_device(): lax.psum_scatter(partial_kv, 'mp', scatter_dimension=1, tiled=True)]
    all_gather x2 -> x0, blocking collectives: 26.1 us -> none  [the longest x1 13.8 us: on_device(): lax.all_gather(grads, 'mp', axis=2, tiled=True).reshape(rows, 2 * inner)]
    unnamed x4 -> x0, waiting for transfers between devices: 18.4 us -> none
    all_to_all x1 -> x0, starting transfers between devices: 11 us -> none  [on_device(): lax.all_to_all(terms, 'pairs', split_axis=0, concat_axis=0, tiled=True)]
    unnamed x12 -> x8, local copies, waits for them, and re-layouts: 7.11 us -> 1.25 us
  transfers between devices with their start and end apart: 4 -> 0, of which waited for: 4 -> 0; matrix products, arithmetic and copies ran while one was open for 4% -> 0% of each run, Pallas kernels for 0% -> 0%
where the time goes in v3:
time: 116 us; the launch traced here: 115 us
  Pallas kernels  111 us (96%)
  matrix products  2.3 us (2%)
  local copies, waits for them, and re-layouts  1.25 us (1%)
    pallas_call x1, Pallas kernels, gather_call(): pl.pallas_call(gather_kernel, out_shape=(jax.ShapeDtypeStruct((CHIPS * LO...  58.9 us
    pallas_call x1, Pallas kernels, finish_call(): pl.pallas_call(finish_kernel, out_shape=(jax.ShapeDtypeStruct((rows, HEAD...  36.7 us
    pallas_call x1, Pallas kernels, pair_call(): pl.pallas_call(pair_kernel, out_shape=(jax.ShapeDtypeStruct((2, CROP, 2 *...  15 us

profile of v3, /device:TPU:6, one launch (start us, length us, event | category | flops | bytes accessed | tf_op | source)
XLA Modules:
  0.0 114.9 jit_solution(5310039788211257061)
XLA Ops:
  0.7 58.9 %shard_map.94 = (bf16[128,192,128]{2,1,0:T(8,128)(2,1)}, bf16[256,1280]{1,0:T(8,128)(2,1)}, s32[8,128]{1,0:T(8,128)}) custom-call(s32[128]{0:T(128)} %len_ref.3, s32[2,1024]{1,0:T(2,128)} %bitcast.15, bf16[256,1280]{1,0:T(8,128)(2,1)} %bitcast.9, bf16[256,1280]{1,0:T(8,128)(2,1)} %bitcast.12, bf16[1280,512]{1,0:T(8,128)(2,1)} %wq_hbm.1, ...), custom_call_target="tpu_custom_call" | custom-call | tf_op jit(solution)/shard_map/pallas_call | solution.py:300
  59.6 15.0 %shard_map.95 = (bf16[2,128,128]{2,1,0:T(8,128)(2,1)}, bf16[2,64,512]{2,1,0:T(8,128)(2,1)}) custom-call(s32[8,128]{1,0:T(8,128)} %get-tuple-element.11.codes_ref, s32[128]{0:T(128)} %len_ref.3, s32[1]{0:T(128)} %bitcast.3.first_ref, bf16[128,192,128]{2,1,0:T(8,128)(2,1)} %get-tuple-element.12.table_hbm), custom_call_target="tpu_custom_call" | custom-call | tf_op jit(solution)/shard_map/pallas_call | solution.py:434
  74.6 0.0 copy-start
  74.6 36.7 %shard_map.96 = (bf16[256,512]{1,0:T(8,128)(2,1)}, f32[8,1280]{1,0:T(8,128)}, f32[8,1280]{1,0:T(8,128)}) custom-call(bf16[2,128,128]{2,1,0:T(8,128)(2,1)} %get-tuple-element.13.hid_ref, bf16[2,64,512]{2,1,0:T(8,128)(2,1)} %get-tuple-element.14.grad_ref, bf16[256,1280]{1,0:T(8,128)(2,1)} %bitcast.10, bf16[256,1280]{1,0:T(8,128)(2,1)} %get-tuple-element.15.sib_hbm), custom_call_target="tpu_custom_call" | custom-call | tf_op jit(solution)/shard_map/pallas_call | solution.py:649
  111.4 0.0 copy-start.2
  111.4 0.0 copy-start.1
  111.4 0.0 copy-done
  111.4 2.3 %convolution_convert_fusion = bf16[256,1280]{1,0:T(8,128)(2,1)} fusion(bf16[256,512]{1,0:T(8,128)(2,1)} %get-tuple-element.16, bf16[512,1280]{1,0:T(8,128)(2,1)S(1)} %copy-done), kind=kOutput, calls=%fused_computation | convolution fusion | flops 335872000 | bytes 2228224 | tf_op jit(solution)/shard_map/dot_general | solution.py:700
  113.7 0.0 copy-done.2
  113.7 0.6 copy.12
  114.3 0.0 copy-done.1
  114.3 0.6 copy.13
Async XLA Ops:
  74.6 36.8 %copy-start = (bf16[512,1280]{1,0:T(8,128)(2,1)S(1)}, bf16[512,1280]{1,0:T(8,128)(2,1)}, u32[]{:S(2)}) copy-start(bf16[512,1280]{1,0:T(8,128)(2,1)} %wo_hbm.1) | copy-start | bytes 3932164
  111.4 2.3 %copy-start.2 = (f32[8,1280]{1,0:T(8,128)S(1)}, f32[8,1280]{1,0:T(8,128)}, u32[]{:S(2)}) copy-start(f32[8,1280]{1,0:T(8,128)} %get-tuple-element.17) | copy-start | bytes 122884
  111.4 2.9 %copy-start.1 = (f32[8,1280]{1,0:T(8,128)S(1)}, f32[8,1280]{1,0:T(8,128)}, u32[]{:S(2)}) copy-start(f32[8,1280]{1,0:T(8,128)} %get-tuple-element.18) | copy-start | bytes 122884

commit v4 on v3

--- a/solution.py
+++ b/solution.py
@@ -17,6 +17,7 @@
 HEADS = 2 * NY
 MESH = pl.DeviceIdType.MESH
 VMEM_LIMIT = 56 * 1024 * 1024
+SCHEDULE = (0, 1, None, 2, 3)
 
 
 def place():
@@ -52,15 +53,16 @@
 
 def gather_kernel(
     len_ref, pairs_ref, emb_hbm, cot_hbm, wq_hbm, wv_hbm, wo_hbm, table_ref, sib_ref, codes_ref,
-    emb, cot, wq, wv, wo, k_send, k_recv, vg_send, vg_recv, block, seed,
+    emb, cot, wq, wv, wo, k_send, k_recv, vg_send, vg_recv, seed,
     lsem, k_ssem, k_rsem, vg_ssem, vg_rsem, bsem, ssem, rsem,
 ):
     z, x, c, y = place()
     mine = y * 2 + c
     sibling = device(z, x, 1 - c, y)
-    partner = device(z, NX - 1 - x, 1 - c, y)
+    above, below = (z + 1) % NZ, (z + NZ - 1) % NZ
     mate = device(z, mate_of(x), c, y)
-    up, down = device((z + 1) % NZ, x, c, y), device((z + NZ - 1) % NZ, x, c, y)
+    up, down = device(above, x, c, y), device(below, x, c, y)
+    mate_up, mate_down = device(above, mate_of(x), c, y), device(below, mate_of(x), c, y)
     col, mate_col = column_of(x, c), column_of(mate_of(x), c)
     sib_col, sib_mate_col = column_of(x, 1 - c), column_of(mate_of(x), 1 - c)
     kept = c == x // 2
@@ -74,12 +76,12 @@
     for load in loads:
         load.start()
     greet(
-        [device(z, x, cd, (y + d) % NY) for d in (1, 2, 3) for cd in (0, 1)] + [sibling, partner, mate, up, down]
+        [device(z, x, cd, (y + d) % NY) for d in (1, 2, 3) for cd in (0, 1)]
+        + [device(z, NX - 1 - x, cd, (y + d) % NY) for d in range(NY) for cd in (0, 1)]
+        + [sibling, mate, up, down, mate_up, mate_down]
     )
     for load in loads:
         load.wait()
-    share = remote(emb, sib_ref, lsem.at[5], lsem.at[6], sibling)
-    share.start()
 
     def copies(j, slot, to):
         return (
@@ -90,113 +92,107 @@
     def project(j):
         rows = slice(j * CROP, (j + 1) * CROP)
 
-        def pieces(yd):
+        def away(step, carry):
+            d = jnp.where(step == 0, 2, jnp.where(step == 1, 1, jnp.where(step == 2, 3, 0)))
+            yd = (y + d) % NY
             at = pl.ds(pl.multiple_of(yd * 2 * HDIM, 2 * HDIM), 2 * HDIM)
             k = jnp.dot(emb[rows], wq[:, at], preferred_element_type=jnp.float32).T
             v = jnp.dot(emb[rows], wv[:, at], preferred_element_type=jnp.float32).T.astype(jnp.bfloat16)
             g = lax.dot_general(cot[rows], wo[at, :], NT, preferred_element_type=jnp.float32).T.astype(jnp.bfloat16)
-            return [
-                (k[cd * HDIM : (cd + 1) * HDIM], v[cd * HDIM : (cd + 1) * HDIM], g[cd * HDIM : (cd + 1) * HDIM])
-                for cd in (0, 1)
-            ]
-
-        def away(step, carry):
-            d = jnp.where(step == 0, 2, jnp.where(step == 1, 1, 3))
-            yd = (y + d) % NY
-            for cd, (k, v, g) in enumerate(pieces(yd)):
-                slot = yd * 2 + cd
-                k_send[j, slot] = k
-                vg_send[j, slot, :HDIM] = v
-                vg_send[j, slot, HDIM:] = g
-                for copy in copies(j, slot, device(z, x, cd, yd)):
-                    copy.start()
+            for h in (0, 1):
+                slot = yd * 2 + h
+                part = slice(h * HDIM, (h + 1) * HDIM)
+                here = kept & (slot == mine)
+
+                @pl.when(here)
+                def _():
+                    k_recv[j, mine] = k[part]
+                    vg_recv[j, mine, :HDIM] = v[part]
+                    vg_recv[j, mine, HDIM:] = g[part]
+
+                @pl.when(jnp.logical_not(here))
+                def _():
+                    k_send[j, slot] = k[part]
+                    vg_send[j, slot, :HDIM] = v[part]
+                    vg_send[j, slot, HDIM:] = g[part]
+                    to = device(z, jnp.where(x // 2 == h, x, NX - 1 - x), x // 2, yd)
+                    for copy in copies(j, slot, to):
+                        copy.start()
+
             return carry
 
-        lax.fori_loop(0, 3, away, 0)
-        both = pieces(y)
-        other = y * 2 + 1 - c
-        k_send[j, other] = jnp.where(c == 0, both[1][0], both[0][0])
-        vg_send[j, other, :HDIM] = jnp.where(c == 0, both[1][1], both[0][1])
-        vg_send[j, other, HDIM:] = jnp.where(c == 0, both[1][2], both[0][2])
-        for copy in copies(j, other, sibling):
-            copy.start()
-        k_recv[j, mine] = jnp.where(c == 0, both[0][0], both[1][0])
-        vg_recv[j, mine, :HDIM] = jnp.where(c == 0, both[0][1], both[1][1])
-        vg_recv[j, mine, HDIM:] = jnp.where(c == 0, both[0][2], both[1][2])
+        lax.fori_loop(0, NY, away, 0)
 
     def settle(j):
-        def arrive(step, carry):
-            slot = (mine + step) % HEADS
-            for copy in (
-                remote(k_recv.at[j, slot], k_recv.at[j, slot], k_ssem.at[j, slot], k_rsem.at[j, slot], sibling),
-                remote(vg_recv.at[j, slot], vg_recv.at[j, slot], vg_ssem.at[j, slot], vg_rsem.at[j, slot], sibling),
-            ):
-                copy.wait_recv()
+        def arrive(slot, carry):
+            @pl.when(jnp.logical_not(kept & (slot == mine)))
+            def _():
+                for ref, ss, rs in ((k_recv, k_ssem, k_rsem), (vg_recv, vg_ssem, vg_rsem)):
+                    remote(ref.at[j, slot], ref.at[j, slot], ss.at[j, slot], rs.at[j, slot], sibling).wait_recv()
+
             return carry
 
-        lax.fori_loop(1, HEADS, arrive, 0)
+        lax.fori_loop(0, HEADS, arrive, 0)
         lanes = lax.broadcasted_iota(jnp.int32, (HDIM, CROP), 1)
-
-        def fill(ref):
-            for cs in (0, 1):
-                k = (k_recv[j, cs] + k_recv[j, 2 + cs]) + (k_recv[j, 4 + cs] + k_recv[j, 6 + cs])
-                vg = [vg_recv[j, 2 * yy + cs].astype(jnp.float32) for yy in range(NY)]
-                vg = (vg[0] + vg[1]) + (vg[2] + vg[3])
-                ok = lanes < len_ref[(z * NX + x) * LOCALS + 2 * cs + j]
-                ref[j, cs, :HDIM] = k.astype(jnp.bfloat16)
-                ref[j, cs, HDIM : 2 * HDIM] = vg[:HDIM].astype(jnp.bfloat16)
-                ref[j, cs, 2 * HDIM :] = jnp.where(ok, vg[HDIM:], 0.0).astype(jnp.bfloat16)
-
-        @pl.when(kept)
-        def _():
-            fill(seed)
-
-        @pl.when(jnp.logical_not(kept))
-        def _():
-            fill(block)
-            swap = remote(block.at[j], seed.at[j], bsem.at[0, j], bsem.at[1, j], partner)
-            swap.start()
-            swap.wait_recv()
-
-        pltpu.make_async_copy(seed.at[j], part(j, z, col), bsem.at[2, j]).start()
-
-    def part(j, bz, bx, half=None):
-        at = j * 2 * CHIPS + (bz * NX + bx) * 2
-        return table_ref.at[pl.ds(at, 2)] if half is None else table_ref.at[pl.ds(at + half, 1)]
-
-    def landed(j, bz, bx, half=None):
-        ref = part(j, bz, bx, half)
-        remote(ref, ref, ssem.at[0], rsem.at[j, bz * NX + bx, half or 0], sibling).wait_recv()
-
-    def spread(j, sent, first):
-        def push(bz, bx, to, half=None, src=None):
-            dst = part(j, bz, bx, half)
-            sem = rsem.at[j, bz * NX + bx, half or 0]
+        for cs in (0, 1):
+            k = (k_recv[j, cs] + k_recv[j, 2 + cs]) + (k_recv[j, 4 + cs] + k_recv[j, 6 + cs])
+            vg = [vg_recv[j, 2 * yy + cs].astype(jnp.float32) for yy in range(NY)]
+            vg = (vg[0] + vg[1]) + (vg[2] + vg[3])
+            ok = lanes < len_ref[(z * NX + col) * LOCALS + 2 * cs + j]
+            seed[j, cs, :HDIM] = k.astype(jnp.bfloat16)
+            seed[j, cs, HDIM : 2 * HDIM] = vg[:HDIM].astype(jnp.bfloat16)
+            seed[j, cs, 2 * HDIM :] = jnp.where(ok, vg[HDIM:], 0.0).astype(jnp.bfloat16)
+        keep(j).start()
+
+    def keep(j):
+        at = pl.ds(j * 2 * CHIPS + (z * NX + col) * 2, 2)
+        return pltpu.make_async_copy(seed.at[j], table_ref.at[at], bsem.at[j])
+
+    def spread(j, cs, sent, first):
+        lane = 2 * j + cs
+
+        def part(bz, bx, half):
+            at = j * 2 * CHIPS + (bz * NX + bx) * 2 + cs
+            if half is None:
+                return table_ref.at[at]
+            return table_ref.at[at, pl.ds(half * 3 * HDIM // 2, 3 * HDIM // 2)]
+
+        def signal(bz, bx, half):
+            return rsem.at[lane, CHIPS + jnp.where(bx == col, 0, 1) if half == 1 else bz * NX + bx]
+
+        def landed(bz, bx, half=None):
+            ref = part(bz, bx, half)
+            remote(ref, ref, ssem.at[0], signal(bz, bx, half), sibling).wait_recv()
+
+        def push(bz, bx, to, half=None, src=None, far=None):
+            dst = part(bz, bx, half)
+            sem = signal(bz, bx, half) if far is None else rsem.at[lane, far]
             copy = remote(dst if src is None else src, dst, ssem.at[len(sent)], sem, to)
             copy.start()
             sent.append(copy)
 
         def hop(s, bx, extra):
             for bz, to, half in (((z + NZ - s) % NZ, up, 0), ((z + s) % NZ, down, 1)):
-                landed(j, bz, bx)
+                landed(bz, bx)
                 push(bz, bx, to, half if s == NZ // 2 - 1 else None)
                 for other in extra:
                     push(bz, bx, other)
 
         def meet(bx, extra):
             bz = (z + NZ // 2) % NZ
-            landed(j, bz, bx, 0)
-            landed(j, bz, bx, 1)
+            landed(bz, bx, 0)
+            landed(bz, bx, 1)
             for other in extra:
                 push(bz, bx, other)
 
         def relay(bz):
-            landed(j, bz, mate_col)
+            landed(bz, mate_col)
             push(bz, mate_col, sibling)
 
+        own = seed.at[j, cs]
         if first == "z":
             for to in (up, down, mate, sibling):
-                push(z, col, to, src=seed.at[j])
+                push(z, col, to, src=own)
             ready = [z]
             yield
             for s in range(1, NZ // 2):
@@ -212,42 +208,43 @@
             relay((z + NZ // 2) % NZ)
             yield
         else:
-            for to in (mate, up, down, sibling):
-                push(z, col, to, src=seed.at[j])
-            yield
-            landed(j, z, mate_col)
-            for to in (up, down, sibling):
-                push(z, mate_col, to)
+            for to in (up, down, mate_up, mate_down, mate, sibling):
+                push(z, col, to, src=own)
             yield
             for s in range(1, NZ // 2):
                 for bx in (col, mate_col):
                     hop(s, bx, (sibling,))
+                if s == 1:
+                    relay(z)
                 yield
             for bx in (col, mate_col):
                 meet(bx, (sibling,))
             yield
+        for bz in range(NZ):
+            landed(bz, sib_col)
+            landed(bz, sib_mate_col)
+        yield
 
     def whole(first):
         sent = []
-        now, later = spread(0, sent, first), spread(1, sent, first)
-        next(now)
-        project(1)
-        next(now)
-        next(now)
-        settle(1)
-        live = [later, now]
+        flows = [spread(j, cs, sent, first) for j in (0, 1) for cs in (0, 1)]
+        for what in SCHEDULE:
+            if what is None:
+                settle(1)
+            else:
+                next(flows[what])
+        live = list(flows)
         while live:
             for one in list(live):
                 if next(one, 1) == 1:
                     live.remove(one)
-        for j in (0, 1):
-            for bz in range(NZ):
-                landed(j, bz, sib_col)
-                landed(j, bz, sib_mate_col)
         for copy in sent:
             copy.wait_send()
 
     project(0)
+    project(1)
+    share = remote(emb, sib_ref, lsem.at[5], lsem.at[6], sibling)
+    share.start()
     first = (z * NX + col) * LOCALS
     a, b = pairs_ref[0:1], pairs_ref[1:2]
     owners = lax.broadcasted_iota(jnp.int32, (8, 1), 0) + first // 2
@@ -275,18 +272,16 @@
 
     for j in (0, 1):
 
-        def leave(step, carry):
-            for copy in copies(j, (mine + step) % HEADS, sibling):
-                copy.wait_send()
+        def leave(slot, carry):
+            @pl.when(jnp.logical_not(kept & (slot == mine)))
+            def _():
+                for copy in copies(j, slot, sibling):
+                    copy.wait_send()
+
             return carry
 
-        lax.fori_loop(1, HEADS, leave, 0)
-        pltpu.make_async_copy(seed.at[j], part(j, z, col), bsem.at[2, j]).wait()
-
-        @pl.when(jnp.logical_not(kept))
-        def _():
-            remote(block.at[j], seed.at[j], bsem.at[0, j], bsem.at[1, j], partner).wait_send()
-
+        lax.fori_loop(0, HEADS, leave, 0)
+        keep(j).wait()
     share.wait()
 
 
@@ -313,15 +308,14 @@
             pltpu.VMEM((2, HEADS, 2 * HDIM, CROP), bf),
             pltpu.VMEM((2, HEADS, 2 * HDIM, CROP), bf),
             pltpu.VMEM((2, 2, 3 * HDIM, CROP), bf),
-            pltpu.VMEM((2, 2, 3 * HDIM, CROP), bf),
             dma((7,)),
             dma((2, HEADS)),
             dma((2, HEADS)),
             dma((2, HEADS)),
             dma((2, HEADS)),
-            dma((3, 2)),
-            dma((72,)),
-            dma((2, CHIPS, 2)),
+            dma((2,)),
+            dma((144,)),
+            dma((LOCALS, CHIPS + 2)),
         ],
         compiler_params=pltpu.CompilerParams(
             collective_id=0, has_side_effects=True, vmem_limit_bytes=VMEM_LIMIT
@@ -686,6 +680,27 @@
     )(hid, grads, emb, sib)
 
 
+def output_kernel(hidden_ref, wo_ref, qk_ref, value_ref, att_ref, out_qk_ref, out_value_ref):
+    att_ref[...] = jnp.dot(hidden_ref[...], wo_ref[...], preferred_element_type=jnp.float32).astype(jnp.bfloat16)
+    out_qk_ref[...] = qk_ref[...]
+    out_value_ref[...] = value_ref[...]
+
+
+def output_call(hidden, w_out, grad_qk, grad_value):
+    vmem = pl.BlockSpec(memory_space=pltpu.VMEM)
+    return pl.pallas_call(
+        output_kernel,
+        out_shape=(
+            jax.ShapeDtypeStruct((hidden.shape[0], w_out.shape[1]), jnp.bfloat16),
+            jax.ShapeDtypeStruct(grad_qk.shape, grad_qk.dtype),
+            jax.ShapeDtypeStruct(grad_value.shape, grad_value.dtype),
+        ),
+        in_specs=[vmem] * 4,
+        out_specs=(vmem,) * 3,
+        compiler_params=pltpu.CompilerParams(vmem_limit_bytes=16 * 1024 * 1024),
+    )(hidden, w_out, grad_qk, grad_value)
+
+
 def on_device(embeddings, cotangent, w_qk, w_value, w_out, lengths, pair_list):
     owned, crop, width = embeddings.shape
     rows = owned * crop
@@ -697,7 +712,7 @@
     )
     hid, grads = pair_call(codes, lengths, first.reshape(1), table)
     hidden, grad_qk, grad_value = finish_call(hid, grads, emb, sib)
-    attended = jnp.dot(hidden, w_out, preferred_element_type=jnp.float32).astype(jnp.bfloat16)
+    attended, grad_qk, grad_value = output_call(hidden, w_out, grad_qk, grad_value)
     return (attended.reshape(embeddings.shape), grad_qk.T, grad_value.T)
 
 

time: 116 us -> 106 us (0.914)
  Pallas kernels: 111 us -> 103 us
  matrix products: 2.3 us -> 0 us
  local copies, waits for them, and re-layouts: 1.25 us -> 2.51 us
    pallas_call x1, Pallas kernels: 58.9 us -> 50.4 us  [gather_call(): pl.pallas_call(gather_kernel, out_shape=(jax.ShapeDtypeStruct((CHIPS * LO...]
    dot_general x1 -> x0, matrix products: 2.3 us -> none  [on_device(): jnp.dot(hidden, w_out, preferred_element_type=jnp.float32)]
    pallas_call x1, Pallas kernels: 15 us -> 13.3 us  [pair_call(): pl.pallas_call(pair_kernel, out_shape=(jax.ShapeDtypeStruct((2, CROP, 2 *...]
    pallas_call x0 -> x1, Pallas kernels: none -> 1.35 us  [output_call(): pl.pallas_call(output_kernel, out_shape=(jax.ShapeDtypeStruct((hidden.sha...]
    unnamed x8, local copies, waits for them, and re-layouts: 1.25 us -> 2.51 us
where the time goes in v4:
time: 106 us
  Pallas kernels  103 us (97%)
  local copies, waits for them, and re-layouts  2.51 us (2%)
    pallas_call x1, Pallas kernels, gather_call(): pl.pallas_call(gather_kernel, out_shape=(jax.ShapeDtypeStruct((CHIPS * LO...  50.4 us
    pallas_call x1, Pallas kernels, finish_call(): pl.pallas_call(finish_kernel, out_shape=(jax.ShapeDtypeStruct((rows, HEAD...  37.5 us
    pallas_call x1, Pallas kernels, pair_call(): pl.pallas_call(pair_kernel, out_shape=(jax.ShapeDtypeStruct((2, CROP, 2 *...  13.3 us
    unnamed x8, local copies, waits for them, and re-layouts  2.51 us

profile of v4, /device:TPU:6, one launch (start us, length us, event | category | flops | bytes accessed | tf_op | source)
XLA Modules:
  0.0 105.8 jit_solution(12672842679809561010)
XLA Ops:
  0.7 50.4 %shard_map.94 = (bf16[128,192,128]{2,1,0:T(8,128)(2,1)}, bf16[256,1280]{1,0:T(8,128)(2,1)}, s32[8,128]{1,0:T(8,128)}) custom-call(s32[128]{0:T(128)} %len_ref.3, s32[2,1024]{1,0:T(2,128)} %bitcast.10, bf16[256,1280]{1,0:T(8,128)(2,1)} %bitcast.7, bf16[256,1280]{1,0:T(8,128)(2,1)} %bitcast.9, bf16[1280,512]{1,0:T(8,128)(2,1)} %wq_hbm.1, ...), custom_call_target="tpu_custom_call" | custom-call | tf_op jit(solution)/shard_map/pallas_call | solution.py:295
  51.1 13.3 %shard_map.95 = (bf16[2,128,128]{2,1,0:T(8,128)(2,1)}, bf16[2,64,512]{2,1,0:T(8,128)(2,1)}) custom-call(s32[8,128]{1,0:T(8,128)} %get-tuple-element.14.codes_ref, s32[128]{0:T(128)} %len_ref.3, s32[1]{0:T(128)} %bitcast.3.first_ref, bf16[128,192,128]{2,1,0:T(8,128)(2,1)} %get-tuple-element.15.table_hbm), custom_call_target="tpu_custom_call" | custom-call | tf_op jit(solution)/shard_map/pallas_call | solution.py:428
  64.4 0.0 copy-start
  64.4 37.5 %shard_map.96 = (bf16[256,512]{1,0:T(8,128)(2,1)}, f32[8,1280]{1,0:T(8,128)}, f32[8,1280]{1,0:T(8,128)}) custom-call(bf16[2,128,128]{2,1,0:T(8,128)(2,1)} %get-tuple-element.16.hid_ref, bf16[2,64,512]{2,1,0:T(8,128)(2,1)} %get-tuple-element.17.grad_ref, bf16[256,1280]{1,0:T(8,128)(2,1)} %bitcast.8, bf16[256,1280]{1,0:T(8,128)(2,1)} %get-tuple-element.18.sib_hbm), custom_call_target="tpu_custom_call" | custom-call | tf_op jit(solution)/shard_map/pallas_call | solution.py:643
  101.9 0.0 copy-done
  101.9 0.0 copy-start.1
  101.9 0.9 copy-done.1
  102.9 0.0 copy-start.2
  102.9 0.8 copy-done.2
  103.7 0.0 copy-start.3
  103.7 0.8 copy-done.3
  104.4 1.3 %shard_map.97 = (bf16[256,1280]{1,0:T(8,128)(2,1)}, f32[8,1280]{1,0:T(8,128)}, f32[8,1280]{1,0:T(8,128)}) custom-call(bf16[256,512]{1,0:T(8,128)(2,1)S(1)} %copy-done.1, bf16[512,1280]{1,0:T(8,128)(2,1)S(1)} %copy-done, f32[8,1280]{1,0:T(8,128)S(1)} %copy-done.2, f32[8,1280]{1,0:T(8,128)S(1)} %copy-done.3), custom_call_target="tpu_custom_call" | custom-call | tf_op jit(solution)/shard_map/pallas_call | solution.py:691
Async XLA Ops:
  64.4 37.5 %copy-start = (bf16[512,1280]{1,0:T(8,128)(2,1)S(1)}, bf16[512,1280]{1,0:T(8,128)(2,1)}, u32[]{:S(2)}) copy-start(bf16[512,1280]{1,0:T(8,128)(2,1)} %wo_ref.1) | copy-start | bytes 3932164
  101.9 1.0 copy-start.1
  102.9 0.8 copy-start.2
  103.7 0.8 copy-start.3

commit v5 on v4

--- a/solution.py
+++ b/solution.py
@@ -15,6 +15,7 @@
 CHIPS = NZ * NX
 LOCALS = 4
 HEADS = 2 * NY
+GROUPS = 20
 MESH = pl.DeviceIdType.MESH
 VMEM_LIMIT = 56 * 1024 * 1024
 SCHEDULE = (0, 1, None, 2, 3)
@@ -257,8 +258,33 @@
         lax.broadcasted_iota(jnp.int32, (count, CROP), 0) // each
         == lax.broadcasted_iota(jnp.int32, (count, CROP), 1)
     ).astype(jnp.float32)
-    codes_ref[...] = jnp.dot(
+    codes = jnp.dot(
         codes.astype(jnp.float32), segment, precision=lax.Precision.HIGHEST, preferred_element_type=jnp.float32
+    )
+    index = lax.broadcasted_iota(jnp.int32, (8, CROP), 0)
+    named = jnp.where(index < 2, codes[0:1], codes[1:2])
+    base = (index * CROP).astype(jnp.float32)
+    member = (named > base) & (named <= base + CROP) & (index < LOCALS)
+    member = member.astype(jnp.float32)
+    before = lax.broadcasted_iota(jnp.int32, (CROP, CROP), 0) < lax.broadcasted_iota(jnp.int32, (CROP, CROP), 1)
+    rank = jnp.dot(member, before.astype(jnp.float32), preferred_element_type=jnp.float32)
+    many = jnp.broadcast_to(jnp.sum(member, axis=1, keepdims=True), (8, CROP))
+    groups = jnp.floor((many + 7.0) * 0.125)
+    start, starts = jnp.zeros((1, CROP), jnp.float32), []
+    for l in range(LOCALS):
+        starts.append(start)
+        start = start + 8.0 * groups[l : l + 1]
+    starts = jnp.concatenate(starts + [start] * 4, axis=0)
+    spot = jnp.where(member > 0, rank + starts, -1.0).T
+    partner = (named - base - 1.0).astype(jnp.bfloat16)
+    across = lax.broadcasted_iota(jnp.int32, (CROP, 2 * CROP), 1).astype(jnp.float32)
+    flat = jnp.zeros((1, 2 * CROP), jnp.float32)
+    for l in range(LOCALS):
+        hot = (spot[:, l : l + 1] == across).astype(jnp.bfloat16)
+        flat = flat + jnp.dot(partner[l : l + 1], hot, preferred_element_type=jnp.float32)
+    zero = jnp.zeros((2, CROP), jnp.float32)
+    codes_ref[...] = jnp.concatenate(
+        [flat[:, :CROP], flat[:, CROP:], zero, many[:LOCALS]], axis=0
     ).astype(jnp.int32)
     settle(0)
 
@@ -324,37 +350,40 @@
 
 
 def pair_kernel(
-    codes_ref, len_ref, first_ref, table_hbm, hid_ref, grad_ref, table_ref, list_ref, count_ref, out_acc, dk_acc, dv_acc, sem
+    lists_ref, len_ref, first_ref, table_hbm, hid_ref, grad_ref, blocks_ref, own_ref, out_acc, dk_acc, dv_acc, sem, own_sem
 ):
-    load = pltpu.make_async_copy(table_hbm, table_ref, sem.at[0])
-    load.start()
-    for l in range(LOCALS + 1):
-        count_ref[l] = 0
-
-    def sort(i, carry):
-        for o in (0, 1):
-            code = codes_ref[o, i]
-            local = jnp.where(code > 0, (code - 1) // CROP, LOCALS)
-            at = count_ref[local]
-            list_ref[local, at] = jnp.maximum(code - 1, 0) % CROP
-            count_ref[local] = at + 1
+    counts = [lists_ref[LOCALS + l, 0] for l in range(LOCALS)]
+    total = sum((count + 7) // 8 for count in counts)
+
+    def spot(p):
+        return (p % 2) * 2 * CHIPS + p // 2
+
+    def partner(group, j):
+        return lists_ref[group // 16, (group % 16) * 8 + j]
+
+    def fetch(group, carry):
+        for j in range(8):
+            pltpu.make_async_copy(
+                table_hbm.at[spot(partner(group, j))], blocks_ref.at[group * 8 + j], sem.at[group]
+            ).start()
         return carry
 
-    lax.fori_loop(0, 2 * CHIPS, sort, 0)
+    def mine(l):
+        return pltpu.make_async_copy(table_hbm.at[spot(first_ref[0] + l)], own_ref.at[l], own_sem.at[l])
+
+    mine(0).start()
+    lax.fori_loop(0, total, fetch, 0)
+    for l in range(1, LOCALS):
+        mine(l).start()
     rows = lax.broadcasted_iota(jnp.int32, (CROP, CROP), 0)
     columns = lax.broadcasted_iota(jnp.int32, (1, CROP), 1)
-    load.wait()
-
-    def spot(p):
-        return (p % 2) * 2 * CHIPS + p // 2
-
+    done = 0
     for l in range(LOCALS):
         me = first_ref[0] + l
         row_bias = jnp.where(rows < len_ref[me], 0.0, -1e30)
-        count = count_ref[l]
-        for extra in range(8):
-            list_ref[l, count + extra] = 0
-        own = table_ref[spot(me)].astype(jnp.float32)
+        count = counts[l]
+        mine(l).wait()
+        own = own_ref[l].astype(jnp.float32)
         kp = own[:HDIM].T.astype(jnp.bfloat16)
         vp = own[HDIM : 2 * HDIM].T.astype(jnp.bfloat16)
         gp = own[2 * HDIM :].T.astype(jnp.bfloat16)
@@ -362,12 +391,14 @@
         dk_acc[...] = jnp.zeros_like(dk_acc)
         dv_acc[...] = jnp.zeros_like(dv_acc)
 
-        def step(base, group):
+        def step(base, group, at):
+            pltpu.make_async_copy(
+                table_hbm.at[pl.ds(0, 8)], blocks_ref.at[pl.ds(at * 8, 8)], sem.at[at]
+            ).wait()
             blocks, lens, live = [], [], []
             for j in range(group):
-                q = list_ref[l, base + j]
-                blocks.append(table_ref[spot(q)])
-                lens.append(len_ref[q])
+                blocks.append(blocks_ref[at * 8 + j])
+                lens.append(len_ref[partner(at, j)])
                 live.append(jnp.where(base + j < count, 1.0, 0.0))
             many = jnp.concatenate(blocks, axis=1)
             kq, vq, gq = many[:HDIM], many[HDIM : 2 * HDIM], many[2 * HDIM :]
@@ -398,16 +429,17 @@
                 )
 
         def eight(i, carry):
-            step(i * 8, 8)
+            step(i * 8, 8, done + i)
             return carry
 
         def four(i, carry):
-            step(big * 8, 4)
+            step(big * 8, 4, done + big)
             return carry
 
         big = (count + 3) // 8
         lax.fori_loop(0, big, eight, 0)
         lax.fori_loop(0, jnp.where(count > big * 8, 1, 0), four, 0)
+        done = done + (count + 7) // 8
         ok = rows[:, :HDIM] < len_ref[me]
         hid_ref[l // 2, :, (l % 2) * HDIM : (l % 2 + 1) * HDIM] = jnp.where(ok, out_acc[...], 0.0).astype(
             jnp.bfloat16
@@ -421,7 +453,7 @@
             grad_ref[core, :, l * CROP : (l + 1) * CROP] = jnp.concatenate(eights, axis=0).astype(jnp.bfloat16)
 
 
-def pair_call(codes, lengths, first, table):
+def pair_call(lists, lengths, first, table):
     smem = pl.BlockSpec(memory_space=pltpu.SMEM)
     vmem = pl.BlockSpec(memory_space=pltpu.VMEM)
     hbm = pl.BlockSpec(memory_space=pl.ANY)
@@ -434,16 +466,16 @@
         in_specs=[smem, smem, smem, hbm],
         out_specs=(vmem, vmem),
         scratch_shapes=[
-            pltpu.VMEM(table.shape, jnp.bfloat16),
-            pltpu.SMEM((LOCALS + 1, 2 * CROP), jnp.int32),
-            pltpu.SMEM((LOCALS + 1,), jnp.int32),
+            pltpu.VMEM((8 * GROUPS, 3 * HDIM, CROP), jnp.bfloat16),
+            pltpu.VMEM((LOCALS, 3 * HDIM, CROP), jnp.bfloat16),
             pltpu.VMEM((CROP, HDIM), jnp.float32),
             pltpu.VMEM((CROP, HDIM), jnp.float32),
             pltpu.VMEM((CROP, HDIM), jnp.float32),
-            pltpu.SemaphoreType.DMA((1,)),
+            pltpu.SemaphoreType.DMA((GROUPS,)),
+            pltpu.SemaphoreType.DMA((LOCALS,)),
         ],
         compiler_params=pltpu.CompilerParams(vmem_limit_bytes=VMEM_LIMIT),
-    )(codes, lengths, first, table)
+    )(lists, lengths, first, table)
 
 
 def ring_sum(n, term, plus, minus, send, recv, ssem, rsem, done):
@@ -528,7 +560,7 @@
     def away(d, cd):
         return jnp.logical_not(kept & (cd == c)) if d == 0 else None
 
-    for kind in (0, 1):
+    def launch(kind):
         for d, cd in ways:
             if d:
                 outgoing(d, cd, kind).start()
@@ -537,6 +569,8 @@
                 @pl.when(away(d, cd))
                 def _():
                     outgoing(d, cd, kind).start()
+
+    launch(0)
 
     @pl.when(kept)
     def _():
@@ -556,6 +590,7 @@
     for load in loads:
         load.wait()
     arrive(g_recv, g_ssem, g_rsem)
+    launch(1)
     width = emb.shape[-1]
     all_g = g_recv[...].reshape(HEADS * HDIM, LOCALS * CROP)
     own = jnp.where(c == 0, all_g[:, : 2 * CROP], all_g[:, 2 * CROP :])
@@ -697,7 +732,7 @@
         ),
         in_specs=[vmem] * 4,
         out_specs=(vmem,) * 3,
-        compiler_params=pltpu.CompilerParams(vmem_limit_bytes=16 * 1024 * 1024),
+        compiler_params=pltpu.CompilerParams(vmem_limit_bytes=VMEM_LIMIT),
     )(hidden, w_out, grad_qk, grad_value)
 
 
@@ -707,10 +742,10 @@
     emb = embeddings.reshape(rows, width)
     z, x, c, _ = place()
     first = LOCALS * (z * NX + column_of(x, c))
-    table, sib, codes = gather_call(
+    table, sib, lists = gather_call(
         lengths, pair_list.T, emb, cotangent.reshape(rows, width), w_qk, w_value, w_out
     )
-    hid, grads = pair_call(codes, lengths, first.reshape(1), table)
+    hid, grads = pair_call(lists, lengths, first.reshape(1), table)
     hidden, grad_qk, grad_value = finish_call(hid, grads, emb, sib)
     attended, grad_qk, grad_value = output_call(hidden, w_out, grad_qk, grad_value)
     return (attended.reshape(embeddings.shape), grad_qk.T, grad_value.T)

time: 106 us -> 105 us (level)
  local copies, waits for them, and re-layouts: 2.51 us -> 0 us
    unnamed x8 -> x0, local copies, waits for them, and re-layouts: 2.51 us -> none
    pallas_call x1, Pallas kernels: 1.35 us -> 2.7 us  [output_call(): pl.pallas_call(output_kernel, out_shape=(jax.ShapeDtypeStruct((hidden.sha...]
    pallas_call x1, Pallas kernels: 37.5 us -> 38.6 us  [finish_call(): pl.pallas_call(finish_kernel, out_shape=(jax.ShapeDtypeStruct((rows, HEAD...]
    pallas_call x1, Pallas kernels: 13.3 us -> 12.1 us  [pair_call(): pl.pallas_call(pair_kernel, out_shape=(jax.ShapeDtypeStruct((2, CROP, 2 *...]
where the time goes in v5:
time: 105 us
  Pallas kernels  104 us (99%)
    pallas_call x1, Pallas kernels, gather_call(): pl.pallas_call(gather_kernel, out_shape=(jax.ShapeDtypeStruct((CHIPS * LO...  50.4 us
    pallas_call x1, Pallas kernels, finish_call(): pl.pallas_call(finish_kernel, out_shape=(jax.ShapeDtypeStruct((rows, HEAD...  38.6 us
    pallas_call x1, Pallas kernels, pair_call(): pl.pallas_call(pair_kernel, out_shape=(jax.ShapeDtypeStruct((2, CROP, 2 *...  12.1 us
    pallas_call x1, Pallas kernels, output_call(): pl.pallas_call(output_kernel, out_shape=(jax.ShapeDtypeStruct((hidden.sha...  2.7 us

profile of v5, /device:TPU:6, one launch (start us, length us, event | category | flops | bytes accessed | tf_op | source)
XLA Modules:
  0.0 104.6 jit_solution(13570834149881721342)
XLA Ops:
  0.7 50.4 %shard_map.94 = (bf16[128,192,128]{2,1,0:T(8,128)(2,1)}, bf16[256,1280]{1,0:T(8,128)(2,1)}, s32[8,128]{1,0:T(8,128)}) custom-call(s32[128]{0:T(128)} %len_ref.3, s32[2,1024]{1,0:T(2,128)} %bitcast.10, bf16[256,1280]{1,0:T(8,128)(2,1)} %bitcast.7, bf16[256,1280]{1,0:T(8,128)(2,1)} %bitcast.9, bf16[1280,512]{1,0:T(8,128)(2,1)} %wq_hbm.1, ...), custom_call_target="tpu_custom_call" | custom-call | tf_op jit(solution)/shard_map/pallas_call | solution.py:321
  51.1 12.1 %shard_map.95 = (bf16[2,128,128]{2,1,0:T(8,128)(2,1)}, bf16[2,64,512]{2,1,0:T(8,128)(2,1)}) custom-call(s32[8,128]{1,0:T(8,128)} %get-tuple-element.14.lists_ref, s32[128]{0:T(128)} %len_ref.3, s32[1]{0:T(128)} %bitcast.3.first_ref, bf16[128,192,128]{2,1,0:T(8,128)(2,1)} %get-tuple-element.15.table_hbm), custom_call_target="tpu_custom_call" | custom-call | tf_op jit(solution)/shard_map/pallas_call | solution.py:460
  63.3 38.6 %shard_map.96 = (bf16[256,512]{1,0:T(8,128)(2,1)}, f32[8,1280]{1,0:T(8,128)}, f32[8,1280]{1,0:T(8,128)}) custom-call(bf16[2,128,128]{2,1,0:T(8,128)(2,1)} %get-tuple-element.16.hid_ref, bf16[2,64,512]{2,1,0:T(8,128)(2,1)} %get-tuple-element.17.grad_ref, bf16[256,1280]{1,0:T(8,128)(2,1)} %bitcast.8, bf16[256,1280]{1,0:T(8,128)(2,1)} %get-tuple-element.18.sib_hbm), custom_call_target="tpu_custom_call" | custom-call | tf_op jit(solution)/shard_map/pallas_call | solution.py:678
  101.9 2.7 %shard_map.97 = (bf16[256,1280]{1,0:T(8,128)(2,1)}, f32[8,1280]{1,0:T(8,128)}, f32[8,1280]{1,0:T(8,128)}) custom-call(bf16[256,512]{1,0:T(8,128)(2,1)} %get-tuple-element.19.hidden_ref, bf16[512,1280]{1,0:T(8,128)(2,1)} %wo_ref.1, f32[8,1280]{1,0:T(8,128)} %get-tuple-element.20.qk_ref, f32[8,1280]{1,0:T(8,128)} %get-tuple-element.21.value_ref), custom_call_target="tpu_custom_call" | custom-call | tf_op jit(solution)/shard_map/pallas_call | solution.py:726

commit v6 on v5

--- a/solution.py
+++ b/solution.py
@@ -518,6 +518,47 @@
     yield
 
 
+def line_sum(term, ways, send, recv, ssem, rsem, done):
+    half = send.shape[-1] // 2
+    whole = slice(None)
+    sent = []
+
+    def copy(way, s, spot, to):
+        return remote(send.at[way, s, :, spot], recv.at[way, s, :, spot], ssem.at[way, s], rsem.at[way, s], to)
+
+    def go(way, s, spot, to):
+        sent.append(copy(way, s, spot, to))
+        sent[-1].start()
+
+    def got(way, s, spot):
+        copy(way, s, spot, ways[way][0]).wait_recv()
+        return recv[way, s, :, spot].astype(jnp.float32)
+
+    for way, (one, two) in enumerate(ways):
+        own = slice(way * half, (way + 1) * half)
+        send[way, 0, :, own] = term(4)[:, own].astype(jnp.bfloat16)
+        go(way, 0, own, two)
+        send[way, 1] = term(3 if way == 0 else 5).astype(jnp.bfloat16)
+        go(way, 1, whole, one)
+    yield
+    for way, (one, two) in enumerate(ways):
+        own = slice(way * half, (way + 1) * half)
+        rest = slice((1 - way) * half, (2 - way) * half)
+        value = term(2 if way == 0 else 6) + got(way, 1, whole)
+        send[way, 2, :, rest] = value[:, rest].astype(jnp.bfloat16)
+        send[way, 2, :, own] = (value[:, own] + got(way, 0, own)).astype(jnp.bfloat16)
+        go(way, 2, whole, one)
+    yield
+    for way, (one, two) in enumerate(ways):
+        send[way, 3] = (term(1 if way == 0 else 7) + got(way, 2, whole)).astype(jnp.bfloat16)
+        go(way, 3, whole, one)
+    yield
+    done(term(0) + got(0, 3, whole) + got(1, 3, whole))
+    for one in sent:
+        one.wait_send()
+    yield
+
+
 def together(*rings):
     live = list(rings)
     while live:
@@ -633,10 +674,9 @@
             def done(total):
                 line[2 * i : 2 * i + 2] = total.reshape(2, 16, width)
 
-            return ring_sum(
-                NZ,
+            return line_sum(
                 lambda d: terms[(z + d) % NZ, 2 * i : 2 * i + 2].reshape(32, width),
-                up, down, z_send.at[i], z_recv.at[i], zs_sem.at[i], zr_sem.at[i], done,
+                ((up, device((z + 2) % NZ, x, c, y)), (down, device((z + NZ - 2) % NZ, x, c, y))), z_send.at[i], z_recv.at[i], zs_sem.at[i], zr_sem.at[i], done,
             )
 
         together(ring(0), ring(1))

time: 105 us -> 103 us (0.981)
  Pallas kernels: 104 us -> 101 us
    pallas_call x1, Pallas kernels: 38.6 us -> 35.6 us  [finish_call(): pl.pallas_call(finish_kernel, out_shape=(jax.ShapeDtypeStruct((rows, HEAD...]
where the time goes in v6:
time: 103 us; the launch traced here: 102 us
  Pallas kernels  101 us (98%)
    pallas_call x1, Pallas kernels, gather_call(): pl.pallas_call(gather_kernel, out_shape=(jax.ShapeDtypeStruct((CHIPS * LO...  50.4 us
    pallas_call x1, Pallas kernels, finish_call(): pl.pallas_call(finish_kernel, out_shape=(jax.ShapeDtypeStruct((rows, HEAD...  35.6 us
    pallas_call x1, Pallas kernels, pair_call(): pl.pallas_call(pair_kernel, out_shape=(jax.ShapeDtypeStruct((2, CROP, 2 *...  12.8 us
    pallas_call x1, Pallas kernels, output_call(): pl.pallas_call(output_kernel, out_shape=(jax.ShapeDtypeStruct((hidden.sha...  2.7 us

profile of v6, /device:TPU:6, one launch (start us, length us, event | category | flops | bytes accessed | tf_op | source)
XLA Modules:
  0.0 102.2 jit_solution(6722345995540313314)
XLA Ops:
  0.7 50.4 %shard_map.94 = (bf16[128,192,128]{2,1,0:T(8,128)(2,1)}, bf16[256,1280]{1,0:T(8,128)(2,1)}, s32[8,128]{1,0:T(8,128)}) custom-call(s32[128]{0:T(128)} %len_ref.3, s32[2,1024]{1,0:T(2,128)} %bitcast.10, bf16[256,1280]{1,0:T(8,128)(2,1)} %bitcast.7, bf16[256,1280]{1,0:T(8,128)(2,1)} %bitcast.9, bf16[1280,512]{1,0:T(8,128)(2,1)} %wq_hbm.1, ...), custom_call_target="tpu_custom_call" | custom-call | tf_op jit(solution)/shard_map/pallas_call | solution.py:321
  51.1 12.8 %shard_map.95 = (bf16[2,128,128]{2,1,0:T(8,128)(2,1)}, bf16[2,64,512]{2,1,0:T(8,128)(2,1)}) custom-call(s32[8,128]{1,0:T(8,128)} %get-tuple-element.14.lists_ref, s32[128]{0:T(128)} %len_ref.3, s32[1]{0:T(128)} %bitcast.3.first_ref, bf16[128,192,128]{2,1,0:T(8,128)(2,1)} %get-tuple-element.15.table_hbm), custom_call_target="tpu_custom_call" | custom-call | tf_op jit(solution)/shard_map/pallas_call | solution.py:460
  63.9 35.6 %shard_map.96 = (bf16[256,512]{1,0:T(8,128)(2,1)}, f32[8,1280]{1,0:T(8,128)}, f32[8,1280]{1,0:T(8,128)}) custom-call(bf16[2,128,128]{2,1,0:T(8,128)(2,1)} %get-tuple-element.16.hid_ref, bf16[2,64,512]{2,1,0:T(8,128)(2,1)} %get-tuple-element.17.grad_ref, bf16[256,1280]{1,0:T(8,128)(2,1)} %bitcast.8, bf16[256,1280]{1,0:T(8,128)(2,1)} %get-tuple-element.18.sib_hbm), custom_call_target="tpu_custom_call" | custom-call | tf_op jit(solution)/shard_map/pallas_call | solution.py:718
  99.5 2.7 %shard_map.97 = (bf16[256,1280]{1,0:T(8,128)(2,1)}, f32[8,1280]{1,0:T(8,128)}, f32[8,1280]{1,0:T(8,128)}) custom-call(bf16[256,512]{1,0:T(8,128)(2,1)} %get-tuple-element.19.hidden_ref, bf16[512,1280]{1,0:T(8,128)(2,1)} %wo_ref.1, f32[8,1280]{1,0:T(8,128)} %get-tuple-element.20.qk_ref, f32[8,1280]{1,0:T(8,128)} %get-tuple-element.21.value_ref), custom_call_target="tpu_custom_call" | custom-call | tf_op jit(solution)/shard_map/pallas_call | solution.py:766

commit v7 on v6

--- a/solution.py
+++ b/solution.py
@@ -16,6 +16,7 @@
 LOCALS = 4
 HEADS = 2 * NY
 GROUPS = 20
+PIECES = 2
 MESH = pl.DeviceIdType.MESH
 VMEM_LIMIT = 56 * 1024 * 1024
 SCHEDULE = (0, 1, None, 2, 3)
@@ -568,8 +569,8 @@
 
 
 def finish_kernel(
-    hid_ref, grad_ref, emb_hbm, sib_hbm, hidden_ref, qk_ref, value_ref,
-    emb, sib, hid_recv, g_recv, terms, z_send, z_recv, x_send, x_recv, line, last_send, last_recv,
+    hid_ref, grad_ref, emb_hbm, sib_hbm, wo_hbm, att_hbm, qk_ref, value_ref,
+    emb, sib, wo, hidden, att, hid_recv, g_recv, terms, z_send, z_recv, x_send, x_recv, line, last_send, last_recv,
     lsem, h_ssem, h_rsem, g_ssem, g_rsem, zs_sem, zr_sem, xs_sem, xr_sem, ls_sem, lr_sem,
 ):
     z, x, c, y = place()
@@ -577,8 +578,11 @@
     kept = c == x // 2
     mine = 2 * y + x // 2
     loads = [pltpu.make_async_copy(emb_hbm, emb, lsem.at[0]), pltpu.make_async_copy(sib_hbm, sib, lsem.at[1])]
+    fetch = pltpu.make_async_copy(wo_hbm, wo, lsem.at[2])
+    store = pltpu.make_async_copy(att, att_hbm, lsem.at[3])
     for load in loads:
         load.start()
+    fetch.start()
     sibling = device(z, x, 1 - c, y)
     up, down = device((z + 1) % NZ, x, c, y), device((z + NZ - 1) % NZ, x, c, y)
     east, west = device(z, (x + 1) % NX, c, y), device(z, (x + NX - 1) % NX, c, y)
@@ -641,6 +645,19 @@
         + jnp.dot(theirs, sib[...], preferred_element_type=jnp.float32)
     ).reshape(terms.shape)
 
+    def heads():
+        arrive(hid_recv, h_ssem, h_rsem)
+        low = lax.broadcasted_iota(jnp.int32, (CROP, 2 * HDIM), 1) < HDIM
+        for yy in range(NY):
+            even = hid_recv[2 * yy].astype(jnp.float32)
+            odd = hid_recv[2 * yy + 1].astype(jnp.float32)
+            at = slice(yy * 2 * HDIM, (yy + 1) * 2 * HDIM)
+            hidden[:CROP, at] = jnp.where(low, even, pltpu.roll(odd, HDIM, 1)).astype(jnp.bfloat16)
+            hidden[CROP:, at] = jnp.where(low, pltpu.roll(even, HDIM, 1), odd).astype(jnp.bfloat16)
+        fetch.wait()
+        att[...] = jnp.dot(hidden[...], wo[...], preferred_element_type=jnp.float32).astype(jnp.bfloat16)
+        store.start()
+
     def finish(n, term, to):
         sends = []
         for d in sorted(range(1, n), key=lambda d: -min(d, n - d)):
@@ -648,6 +665,7 @@
             copy = remote(last_send.at[d], last_recv.at[d], ls_sem.at[d], lr_sem.at[d], to(d))
             copy.start()
             sends.append(copy)
+        heads()
         total = term(0)
         for copy in sends:
             copy.wait_recv()
@@ -658,28 +676,18 @@
         for copy in sends:
             copy.wait_send()
 
-    def heads():
-        arrive(hid_recv, h_ssem, h_rsem)
-        low = lax.broadcasted_iota(jnp.int32, (CROP, 2 * HDIM), 1) < HDIM
-        for yy in range(NY):
-            even = hid_recv[2 * yy].astype(jnp.float32)
-            odd = hid_recv[2 * yy + 1].astype(jnp.float32)
-            at = slice(yy * 2 * HDIM, (yy + 1) * 2 * HDIM)
-            hidden_ref[:CROP, at] = jnp.where(low, even, pltpu.roll(odd, HDIM, 1)).astype(jnp.bfloat16)
-            hidden_ref[CROP:, at] = jnp.where(low, pltpu.roll(even, HDIM, 1), odd).astype(jnp.bfloat16)
-
     @pl.when(c == 0)
     def _():
         def ring(i):
             def done(total):
-                line[2 * i : 2 * i + 2] = total.reshape(2, 16, width)
+                line[i] = total
 
             return line_sum(
-                lambda d: terms[(z + d) % NZ, 2 * i : 2 * i + 2].reshape(32, width),
+                lambda d: terms[(z + d) % NZ, i],
                 ((up, device((z + 2) % NZ, x, c, y)), (down, device((z + NZ - 2) % NZ, x, c, y))), z_send.at[i], z_recv.at[i], zs_sem.at[i], zr_sem.at[i], done,
             )
 
-        together(ring(0), ring(1))
+        together(*[ring(i) for i in range(NX)])
         finish(NX, lambda d: line[(x + d) % NX], lambda d: device(z, (x + d) % NX, c, y))
 
     @pl.when(c == 1)
@@ -697,7 +705,7 @@
         together(ring(0), ring(1))
         finish(NZ, lambda d: line[(z + d) % NZ], lambda d: device((z + d) % NZ, x, c, y))
 
-    heads()
+    store.wait()
     for d, cd in ways:
         for kind in (0, 1):
             if d:
@@ -709,7 +717,7 @@
                     outgoing(d, cd, kind).wait_send()
 
 
-def finish_call(hid, grads, emb, sib):
+def finish_call(hid, grads, emb, sib, w_out):
     rows, width = emb.shape
     vmem = pl.BlockSpec(memory_space=pltpu.VMEM)
     hbm = pl.BlockSpec(memory_space=pl.ANY)
@@ -718,32 +726,35 @@
     return pl.pallas_call(
         finish_kernel,
         out_shape=(
-            jax.ShapeDtypeStruct((rows, HEADS * HDIM), bf),
+            jax.ShapeDtypeStruct((rows, width), bf),
             jax.ShapeDtypeStruct((8, width), jnp.float32),
             jax.ShapeDtypeStruct((8, width), jnp.float32),
         ),
-        in_specs=[vmem, vmem, hbm, hbm],
-        out_specs=(vmem, vmem, vmem),
+        in_specs=[vmem, vmem, hbm, hbm, hbm],
+        out_specs=(hbm, vmem, vmem),
         scratch_shapes=[
             pltpu.VMEM((rows, width), bf),
+            pltpu.VMEM((rows, width), bf),
+            pltpu.VMEM(w_out.shape, bf),
+            pltpu.VMEM((rows, w_out.shape[0]), bf),
             pltpu.VMEM((rows, width), bf),
             pltpu.VMEM((HEADS, CROP, 2 * HDIM), bf),
             pltpu.VMEM((HEADS, HDIM, LOCALS * CROP), bf),
             pltpu.VMEM((NZ, NX, 16, width), jnp.float32),
-            pltpu.VMEM((2, 2, NZ // 2, 32, width), bf),
-            pltpu.VMEM((2, 2, NZ // 2, 32, width), bf),
+            pltpu.VMEM((NX, 2, NZ // 2, 16, width), bf),
+            pltpu.VMEM((NX, 2, NZ // 2, 16, width), bf),
             pltpu.VMEM((2, 2, NX // 2, 64, width), bf),
             pltpu.VMEM((2, 2, NX // 2, 64, width), bf),
             pltpu.VMEM((NZ, 16, width), jnp.float32),
             pltpu.VMEM((NZ, 16, width), bf),
             pltpu.VMEM((NZ, 16, width), bf),
-            dma((2,)),
+            dma((4,)),
             dma((HEADS,)),
             dma((HEADS,)),
             dma((HEADS,)),
             dma((HEADS,)),
-            dma((2, 2, NZ // 2)),
-            dma((2, 2, NZ // 2)),
+            dma((NX, 2, NZ // 2)),
+            dma((NX, 2, NZ // 2)),
             dma((2, 2, NX // 2)),
             dma((2, 2, NX // 2)),
             dma((NZ,)),
@@ -752,28 +763,37 @@
         compiler_params=pltpu.CompilerParams(
             collective_id=1, has_side_effects=True, vmem_limit_bytes=VMEM_LIMIT
         ),
-    )(hid, grads, emb, sib)
-
-
-def output_kernel(hidden_ref, wo_ref, qk_ref, value_ref, att_ref, out_qk_ref, out_value_ref):
-    att_ref[...] = jnp.dot(hidden_ref[...], wo_ref[...], preferred_element_type=jnp.float32).astype(jnp.bfloat16)
-    out_qk_ref[...] = qk_ref[...]
-    out_value_ref[...] = value_ref[...]
-
-
-def output_call(hidden, w_out, grad_qk, grad_value):
-    vmem = pl.BlockSpec(memory_space=pltpu.VMEM)
+    )(hid, grads, emb, sib, w_out)
+
+
+def output_kernel(att_ref, qk_ref, value_ref, out_att_ref, out_qk_ref, out_value_ref, att, qk, value, sem):
+    rows = att.shape[0] // PIECES
+    moves = [(qk_ref, qk, out_qk_ref), (value_ref, value, out_value_ref)]
+    for i in range(PIECES):
+        part = pl.ds(i * rows, rows)
+        moves.append((att_ref.at[part], att.at[part], out_att_ref.at[part]))
+    come = [pltpu.make_async_copy(src, mid, sem.at[0, i]) for i, (src, mid, dst) in enumerate(moves)]
+    go = [pltpu.make_async_copy(mid, dst, sem.at[1, i]) for i, (src, mid, dst) in enumerate(moves)]
+    for copy in come:
+        copy.start()
+    for first, then in zip(come, go):
+        first.wait()
+        then.start()
+    for copy in go:
+        copy.wait()
+
+
+def output_call(*results):
+    hbm = pl.BlockSpec(memory_space=pl.ANY)
     return pl.pallas_call(
         output_kernel,
-        out_shape=(
-            jax.ShapeDtypeStruct((hidden.shape[0], w_out.shape[1]), jnp.bfloat16),
-            jax.ShapeDtypeStruct(grad_qk.shape, grad_qk.dtype),
-            jax.ShapeDtypeStruct(grad_value.shape, grad_value.dtype),
-        ),
-        in_specs=[vmem] * 4,
-        out_specs=(vmem,) * 3,
+        out_shape=tuple(jax.ShapeDtypeStruct(v.shape, v.dtype) for v in results),
+        in_specs=[hbm] * 3,
+        out_specs=(hbm,) * 3,
+        scratch_shapes=[pltpu.VMEM(v.shape, v.dtype) for v in results]
+        + [pltpu.SemaphoreType.DMA((2, PIECES + 2))],
         compiler_params=pltpu.CompilerParams(vmem_limit_bytes=VMEM_LIMIT),
-    )(hidden, w_out, grad_qk, grad_value)
+    )(*results)
 
 
 def on_device(embeddings, cotangent, w_qk, w_value, w_out, lengths, pair_list):
@@ -786,8 +806,7 @@
         lengths, pair_list.T, emb, cotangent.reshape(rows, width), w_qk, w_value, w_out
     )
     hid, grads = pair_call(lists, lengths, first.reshape(1), table)
-    hidden, grad_qk, grad_value = finish_call(hid, grads, emb, sib)
-    attended, grad_qk, grad_value = output_call(hidden, w_out, grad_qk, grad_value)
+    attended, grad_qk, grad_value = output_call(*finish_call(hid, grads, emb, sib, w_out))
     return (attended.reshape(embeddings.shape), grad_qk.T, grad_value.T)
 
 

time: 103 us -> 100 us (0.971)
  Pallas kernels: 101 us -> 98.5 us
    pallas_call x2, Pallas kernels: 38.3 us -> 35.3 us  [the longest x1 33.4 us: finish_call(): pl.pallas_call(finish_kernel, out_shape=(jax.ShapeDtypeStruct((rows, widt...]
where the time goes in v7:
time: 100 us; the launch traced here: 99.4 us
  Pallas kernels  98.5 us (98%)
    pallas_call x1, Pallas kernels, gather_call(): pl.pallas_call(gather_kernel, out_shape=(jax.ShapeDtypeStruct((CHIPS * LO...  50.4 us
    pallas_call x1, Pallas kernels, finish_call(): pl.pallas_call(finish_kernel, out_shape=(jax.ShapeDtypeStruct((rows, widt...  33.4 us
    pallas_call x1, Pallas kernels, pair_call(): pl.pallas_call(pair_kernel, out_shape=(jax.ShapeDtypeStruct((2, CROP, 2 *...  12.8 us

profile of v7, /device:TPU:6, one launch (start us, length us, event | category | flops | bytes accessed | tf_op | source)
XLA Modules:
  0.0 99.4 jit_solution(16088212148457415406)
XLA Ops:
  0.7 50.4 %shard_map.94 = (bf16[128,192,128]{2,1,0:T(8,128)(2,1)}, bf16[256,1280]{1,0:T(8,128)(2,1)}, s32[8,128]{1,0:T(8,128)}) custom-call(s32[128]{0:T(128)} %len_ref.3, s32[2,1024]{1,0:T(2,128)} %bitcast.10, bf16[256,1280]{1,0:T(8,128)(2,1)} %bitcast.7, bf16[256,1280]{1,0:T(8,128)(2,1)} %bitcast.9, bf16[1280,512]{1,0:T(8,128)(2,1)} %wq_hbm.1, ...), custom_call_target="tpu_custom_call" | custom-call | tf_op jit(solution)/shard_map/pallas_call | solution.py:322
  51.1 12.8 %shard_map.95 = (bf16[2,128,128]{2,1,0:T(8,128)(2,1)}, bf16[2,64,512]{2,1,0:T(8,128)(2,1)}) custom-call(s32[8,128]{1,0:T(8,128)} %get-tuple-element.14.lists_ref, s32[128]{0:T(128)} %len_ref.3, s32[1]{0:T(128)} %bitcast.3.first_ref, bf16[128,192,128]{2,1,0:T(8,128)(2,1)} %get-tuple-element.15.table_hbm), custom_call_target="tpu_custom_call" | custom-call | tf_op jit(solution)/shard_map/pallas_call | solution.py:461
  63.9 33.4 %shard_map.96 = (bf16[256,1280]{1,0:T(8,128)(2,1)}, f32[8,1280]{1,0:T(8,128)}, f32[8,1280]{1,0:T(8,128)}) custom-call(bf16[2,128,128]{2,1,0:T(8,128)(2,1)} %get-tuple-element.16.hid_ref, bf16[2,64,512]{2,1,0:T(8,128)(2,1)} %get-tuple-element.17.grad_ref, bf16[256,1280]{1,0:T(8,128)(2,1)} %bitcast.8, bf16[256,1280]{1,0:T(8,128)(2,1)} %get-tuple-element.18.sib_hbm, ...), custom_call_target="tpu_custom_call" | custom-call | tf_op jit(solution)/shard_map/pallas_call | solution.py:726
  97.3 1.9 %shard_map.97 = (bf16[256,1280]{1,0:T(8,128)(2,1)}, f32[8,1280]{1,0:T(8,128)}, f32[8,1280]{1,0:T(8,128)}) custom-call(bf16[256,1280]{1,0:T(8,128)(2,1)} %get-tuple-element.19.att_ref, f32[8,1280]{1,0:T(8,128)} %get-tuple-element.20.qk_ref, f32[8,1280]{1,0:T(8,128)} %get-tuple-element.21.value_ref), custom_call_target="tpu_custom_call" | custom-call | tf_op jit(solution)/shard_map/pallas_call | solution.py:788

commit v8 on v7

--- a/solution.py
+++ b/solution.py
@@ -199,6 +199,7 @@
             yield
             for s in range(1, NZ // 2):
                 hop(s, col, (mate, sibling))
+                yield
                 for bz in ready:
                     relay(bz)
                 ready = [(z + NZ - s) % NZ, (z + s) % NZ]
@@ -658,12 +659,16 @@
         att[...] = jnp.dot(hidden[...], wo[...], preferred_element_type=jnp.float32).astype(jnp.bfloat16)
         store.start()
 
-    def finish(n, term, to):
+    def last(d, to):
+        return remote(last_send.at[d], last_recv.at[d], ls_sem.at[d], lr_sem.at[d], to)
+
+    def finish(n, term, to, sent=False):
         sends = []
         for d in sorted(range(1, n), key=lambda d: -min(d, n - d)):
-            last_send[d] = term(d).astype(jnp.bfloat16)
-            copy = remote(last_send.at[d], last_recv.at[d], ls_sem.at[d], lr_sem.at[d], to(d))
-            copy.start()
+            copy = last(d, to(d))
+            if not sent:
+                last_send[d] = term(d).astype(jnp.bfloat16)
+                copy.start()
             sends.append(copy)
         heads()
         total = term(0)
@@ -681,6 +686,12 @@
         def ring(i):
             def done(total):
                 line[i] = total
+                d = (i + NX - x) % NX
+
+                @pl.when(d != 0)
+                def _():
+                    last_send[d] = total.astype(jnp.bfloat16)
+                    last(d, device(z, i, c, y)).start()
 
             return line_sum(
                 lambda d: terms[(z + d) % NZ, i],
@@ -688,7 +699,7 @@
             )
 
         together(*[ring(i) for i in range(NX)])
-        finish(NX, lambda d: line[(x + d) % NX], lambda d: device(z, (x + d) % NX, c, y))
+        finish(NX, lambda d: line[(x + d) % NX], lambda d: device(z, (x + d) % NX, c, y), sent=True)
 
     @pl.when(c == 1)
     def _():

time: 100 us -> 101 us (1.010)
  Pallas kernels: 98.5 us -> 99.7 us
    pallas_call x1, Pallas kernels: 33.4 us -> 34.8 us  [finish_call(): pl.pallas_call(finish_kernel, out_shape=(jax.ShapeDtypeStruct((rows, widt...]
where the time goes in v8:
time: 101 us
  Pallas kernels  99.7 us (99%)
    pallas_call x1, Pallas kernels, gather_call(): pl.pallas_call(gather_kernel, out_shape=(jax.ShapeDtypeStruct((CHIPS * LO...  50.4 us
    pallas_call x1, Pallas kernels, finish_call(): pl.pallas_call(finish_kernel, out_shape=(jax.ShapeDtypeStruct((rows, widt...  34.8 us
    pallas_call x1, Pallas kernels, pair_call(): pl.pallas_call(pair_kernel, out_shape=(jax.ShapeDtypeStruct((2, CROP, 2 *...  12.5 us

profile of v8, /device:TPU:6, one launch (start us, length us, event | category | flops | bytes accessed | tf_op | source)
XLA Modules:
  0.0 100.6 jit_solution(3560954489811174216)
XLA Ops:
  0.7 50.4 %shard_map.94 = (bf16[128,192,128]{2,1,0:T(8,128)(2,1)}, bf16[256,1280]{1,0:T(8,128)(2,1)}, s32[8,128]{1,0:T(8,128)}) custom-call(s32[128]{0:T(128)} %len_ref.3, s32[2,1024]{1,0:T(2,128)} %bitcast.10, bf16[256,1280]{1,0:T(8,128)(2,1)} %bitcast.7, bf16[256,1280]{1,0:T(8,128)(2,1)} %bitcast.9, bf16[1280,512]{1,0:T(8,128)(2,1)} %wq_hbm.1, ...), custom_call_target="tpu_custom_call" | custom-call | tf_op jit(solution)/shard_map/pallas_call | solution.py:323
  51.1 12.5 %shard_map.95 = (bf16[2,128,128]{2,1,0:T(8,128)(2,1)}, bf16[2,64,512]{2,1,0:T(8,128)(2,1)}) custom-call(s32[8,128]{1,0:T(8,128)} %get-tuple-element.14.lists_ref, s32[128]{0:T(128)} %len_ref.3, s32[1]{0:T(128)} %bitcast.3.first_ref, bf16[128,192,128]{2,1,0:T(8,128)(2,1)} %get-tuple-element.15.table_hbm), custom_call_target="tpu_custom_call" | custom-call | tf_op jit(solution)/shard_map/pallas_call | solution.py:462
  63.7 34.8 %shard_map.96 = (bf16[256,1280]{1,0:T(8,128)(2,1)}, f32[8,1280]{1,0:T(8,128)}, f32[8,1280]{1,0:T(8,128)}) custom-call(bf16[2,128,128]{2,1,0:T(8,128)(2,1)} %get-tuple-element.16.hid_ref, bf16[2,64,512]{2,1,0:T(8,128)(2,1)} %get-tuple-element.17.grad_ref, bf16[256,1280]{1,0:T(8,128)(2,1)} %bitcast.8, bf16[256,1280]{1,0:T(8,128)(2,1)} %get-tuple-element.18.sib_hbm, ...), custom_call_target="tpu_custom_call" | custom-call | tf_op jit(solution)/shard_map/pallas_call | solution.py:737
  98.5 1.9 %shard_map.97 = (bf16[256,1280]{1,0:T(8,128)(2,1)}, f32[8,1280]{1,0:T(8,128)}, f32[8,1280]{1,0:T(8,128)}) custom-call(bf16[256,1280]{1,0:T(8,128)(2,1)} %get-tuple-element.19.att_ref, f32[8,1280]{1,0:T(8,128)} %get-tuple-element.20.qk_ref, f32[8,1280]{1,0:T(8,128)} %get-tuple-element.21.value_ref), custom_call_target="tpu_custom_call" | custom-call | tf_op jit(solution)/shard_map/pallas_call | solution.py:799

commit v9 on v8

--- a/solution.py
+++ b/solution.py
@@ -19,7 +19,6 @@
 PIECES = 2
 MESH = pl.DeviceIdType.MESH
 VMEM_LIMIT = 56 * 1024 * 1024
-SCHEDULE = (0, 1, None, 2, 3)
 
 
 def place():
@@ -125,8 +124,10 @@
 
         lax.fori_loop(0, NY, away, 0)
 
-    def settle(j):
-        def arrive(slot, carry):
+    def settle(j, cs):
+        def arrive(yy, carry):
+            slot = 2 * yy + cs
+
             @pl.when(jnp.logical_not(kept & (slot == mine)))
             def _():
                 for ref, ss, rs in ((k_recv, k_ssem, k_rsem), (vg_recv, vg_ssem, vg_rsem)):
@@ -134,17 +135,17 @@
 
             return carry
 
-        lax.fori_loop(0, HEADS, arrive, 0)
+        lax.fori_loop(0, NY, arrive, 0)
         lanes = lax.broadcasted_iota(jnp.int32, (HDIM, CROP), 1)
-        for cs in (0, 1):
-            k = (k_recv[j, cs] + k_recv[j, 2 + cs]) + (k_recv[j, 4 + cs] + k_recv[j, 6 + cs])
-            vg = [vg_recv[j, 2 * yy + cs].astype(jnp.float32) for yy in range(NY)]
-            vg = (vg[0] + vg[1]) + (vg[2] + vg[3])
-            ok = lanes < len_ref[(z * NX + col) * LOCALS + 2 * cs + j]
-            seed[j, cs, :HDIM] = k.astype(jnp.bfloat16)
-            seed[j, cs, HDIM : 2 * HDIM] = vg[:HDIM].astype(jnp.bfloat16)
-            seed[j, cs, 2 * HDIM :] = jnp.where(ok, vg[HDIM:], 0.0).astype(jnp.bfloat16)
-        keep(j).start()
+        k = (k_recv[j, cs] + k_recv[j, 2 + cs]) + (k_recv[j, 4 + cs] + k_recv[j, 6 + cs])
+        vg = [vg_recv[j, 2 * yy + cs].astype(jnp.float32) for yy in range(NY)]
+        vg = (vg[0] + vg[1]) + (vg[2] + vg[3])
+        ok = lanes < len_ref[(z * NX + col) * LOCALS + 2 * cs + j]
+        seed[j, cs, :HDIM] = k.astype(jnp.bfloat16)
+        seed[j, cs, HDIM : 2 * HDIM] = vg[:HDIM].astype(jnp.bfloat16)
+        seed[j, cs, 2 * HDIM :] = jnp.where(ok, vg[HDIM:], 0.0).astype(jnp.bfloat16)
+        if cs == 1:
+            keep(j).start()
 
     def keep(j):
         at = pl.ds(j * 2 * CHIPS + (z * NX + col) * 2, 2)
@@ -231,11 +232,11 @@
     def whole(first):
         sent = []
         flows = [spread(j, cs, sent, first) for j in (0, 1) for cs in (0, 1)]
-        for what in SCHEDULE:
-            if what is None:
-                settle(1)
-            else:
-                next(flows[what])
+        for j in (0, 1):
+            for cs in (0, 1):
+                if j or cs:
+                    settle(j, cs)
+                next(flows[2 * j + cs])
         live = list(flows)
         while live:
             for one in list(live):
@@ -288,7 +289,7 @@
     codes_ref[...] = jnp.concatenate(
         [flat[:, :CROP], flat[:, CROP:], zero, many[:LOCALS]], axis=0
     ).astype(jnp.int32)
-    settle(0)
+    settle(0, 0)
 
     @pl.when(c == 0)
     def _():

time: 101 us -> 99.8 us (0.988)
  no operation moved by 1% of the time
where the time goes in v9:
time: 99.8 us
  Pallas kernels  98.9 us (99%)
    pallas_call x1, Pallas kernels, gather_call(): pl.pallas_call(gather_kernel, out_shape=(jax.ShapeDtypeStruct((CHIPS * LO...  50.4 us
    pallas_call x1, Pallas kernels, finish_call(): pl.pallas_call(finish_kernel, out_shape=(jax.ShapeDtypeStruct((rows, widt...  33.9 us
    pallas_call x1, Pallas kernels, pair_call(): pl.pallas_call(pair_kernel, out_shape=(jax.ShapeDtypeStruct((2, CROP, 2 *...  12.8 us

profile of v9, /device:TPU:6, one launch (start us, length us, event | category | flops | bytes accessed | tf_op | source)
XLA Modules:
  0.0 99.8 jit_solution(12920914504869527067)
XLA Ops:
  0.7 50.4 %shard_map.94 = (bf16[128,192,128]{2,1,0:T(8,128)(2,1)}, bf16[256,1280]{1,0:T(8,128)(2,1)}, s32[8,128]{1,0:T(8,128)}) custom-call(s32[128]{0:T(128)} %len_ref.3, s32[2,1024]{1,0:T(2,128)} %bitcast.10, bf16[256,1280]{1,0:T(8,128)(2,1)} %bitcast.7, bf16[256,1280]{1,0:T(8,128)(2,1)} %bitcast.9, bf16[1280,512]{1,0:T(8,128)(2,1)} %wq_hbm.1, ...), custom_call_target="tpu_custom_call" | custom-call | tf_op jit(solution)/shard_map/pallas_call | solution.py:324
  51.1 12.8 %shard_map.95 = (bf16[2,128,128]{2,1,0:T(8,128)(2,1)}, bf16[2,64,512]{2,1,0:T(8,128)(2,1)}) custom-call(s32[8,128]{1,0:T(8,128)} %get-tuple-element.14.lists_ref, s32[128]{0:T(128)} %len_ref.3, s32[1]{0:T(128)} %bitcast.3.first_ref, bf16[128,192,128]{2,1,0:T(8,128)(2,1)} %get-tuple-element.15.table_hbm), custom_call_target="tpu_custom_call" | custom-call | tf_op jit(solution)/shard_map/pallas_call | solution.py:463
  63.9 33.9 %shard_map.96 = (bf16[256,1280]{1,0:T(8,128)(2,1)}, f32[8,1280]{1,0:T(8,128)}, f32[8,1280]{1,0:T(8,128)}) custom-call(bf16[2,128,128]{2,1,0:T(8,128)(2,1)} %get-tuple-element.16.hid_ref, bf16[2,64,512]{2,1,0:T(8,128)(2,1)} %get-tuple-element.17.grad_ref, bf16[256,1280]{1,0:T(8,128)(2,1)} %bitcast.8, bf16[256,1280]{1,0:T(8,128)(2,1)} %get-tuple-element.18.sib_hbm, ...), custom_call_target="tpu_custom_call" | custom-call | tf_op jit(solution)/shard_map/pallas_call | solution.py:738
  97.7 1.9 %shard_map.97 = (bf16[256,1280]{1,0:T(8,128)(2,1)}, f32[8,1280]{1,0:T(8,128)}, f32[8,1280]{1,0:T(8,128)}) custom-call(bf16[256,1280]{1,0:T(8,128)(2,1)} %get-tuple-element.19.att_ref, f32[8,1280]{1,0:T(8,128)} %get-tuple-element.20.qk_ref, f32[8,1280]{1,0:T(8,128)} %get-tuple-element.21.value_ref), custom_call_target="tpu_custom_call" | custom-call | tf_op jit(solution)/shard_map/pallas_call | solution.py:800
